TPU v7x, 256 devices: a whole 4x4x8 slice. The times are simulated.
256 devices in a mesh: tm: 32 (over z, x), tmpl: 8 (over y, core).
Axes of the slice: x: 4, y: 4, z: 8, core: 2. Of those that a mesh axis runs over, the one named last changes fastest.
Arguments:
- strain: float32 [2, 3, 4194304], P(None, None, 'tm'), may hold values from -6 to 6
- templates: float32 [2, 8, 2048, 2048], P(None, 'tmpl', 'tm'), may hold values from -6 to 6
- pattern: int32 [8, 1024], P('tmpl'), may hold values 0 or 1
- cutoff: int32 [8], P('tmpl'), may hold values from 256 to 1024
Outputs:
- snr_power: float32 [8, 4194304], P('tmpl', 'tm')
- bank_peak: float32 [4194304], P('tm')
All inputs are finite; a program needn't handle non-finite values. No bound on the sum of `pattern` on one device may be relied on, other than what follows from the above.
Results may differ from a plain program's by a relative error of at most 0.000092.
Values sent between devices are 32-bit elements; how exact they have to be, the bound alone decides.
No kernel may reach another device: no remote copies, remote signals or barrier semaphores. Data moves between devices by JAX's collectives and lax.ppermute only.
A program may use at most 128 MiB of HBM per device.

v0:
```python
import functools
import math

import jax
import jax.numpy as jnp
import numpy as np
from jax import lax
from jax.experimental import pallas as pl
from jax.experimental.pallas import tpu as pltpu
from jax.sharding import PartitionSpec as P

EPSILON = 1e-06
SIDE = 2048
FULL = SIDE * SIDE
DETECTORS = 3
RANKS = 32
GROUPS = 8
F32 = jnp.float32
BF16 = jnp.bfloat16
VMEM_LIMIT = 56 * 1024 * 1024


def split_table(table):
    high = table.astype(np.float32).astype(jnp.bfloat16)
    low = (table - high.astype(np.float64)).astype(np.float32).astype(jnp.bfloat16)
    return np.stack((high, low))


def first_table(copies):
    theta = 2.0 * np.pi * np.outer(np.arange(64), np.arange(64)) / 64.0
    eye = np.eye(copies)
    cosine, sine = np.kron(eye, np.cos(theta)), np.kron(eye, np.sin(theta))
    return split_table(np.block([[cosine, -sine], [sine, cosine]]))


def last_table():
    theta = 2.0 * np.pi * np.outer(np.arange(16), np.arange(16)) / 16.0
    eye = np.eye(8)
    cosine, sine = np.kron(eye, np.cos(theta)), np.kron(eye, np.sin(theta))
    return split_table(np.block([[cosine, sine], [-sine, cosine]]))


def column_table():
    theta = 2.0 * np.pi * np.outer(np.arange(128), np.arange(128)) / 128.0
    cosine, sine = np.cos(theta), np.sin(theta)
    whole = np.block([[cosine, sine], [-sine, cosine]])
    return np.stack((split_table(whole), split_table(whole.T)))


def digit_twiddle():
    digit = 2 * np.arange(8)[:, None, None] + (np.arange(128) // 64)[None, None, :]
    theta = 2.0 * np.pi * (np.arange(128)[None, :, None] * digit) / SIDE
    return np.stack((np.cos(theta), np.sin(theta)), axis=1).astype(np.float32)


def fold_twiddle():
    theta = 2.0 * np.pi * np.outer(np.arange(8), np.arange(128) // 64) / 16.0
    return np.stack((np.cos(theta), -np.sin(theta)), axis=1).astype(np.float32)


def row_twiddle():
    theta = 2.0 * np.pi * np.outer(np.arange(32), np.arange(128) % 64) / SIDE
    return np.stack((np.cos(theta), np.sin(theta))).astype(np.float32)


def inner_twiddle():
    theta = 2.0 * np.pi * np.outer(np.arange(32), np.arange(128) % 16) / 512.0
    return np.stack((np.cos(theta), np.sin(theta))).astype(np.float32)


def phases(turns, orient):
    angle = (turns % FULL).astype(F32) * (orient * 2.0 * math.pi / FULL)
    return jnp.stack((jnp.cos(angle), jnp.sin(angle)))


def mixing_tables(place):
    k = jnp.arange(8, dtype=jnp.int32)[:, None, None]
    into = jnp.arange(128, dtype=jnp.int32)[None, :, None]
    out = jnp.arange(128, dtype=jnp.int32)[None, None, :]
    block, w = k + 8 * (out // 64), out // 16 % 4
    e, a, i = into // 64, into // 16 % 4, into % 16
    turns = e * block * (FULL // 16) + 128 * block * (512 * a + 16 * place + i)
    turns = turns % FULL + a * w * (FULL // 4) + (16 * place + i) * w * SIDE
    cosine, sine = phases(turns, 1.0) * (i == out % 16).astype(F32)
    whole = jnp.concatenate(
        (jnp.concatenate((cosine, sine), axis=2), jnp.concatenate((-sine, cosine), axis=2)), axis=1
    )
    high = lax.reduce_precision(whole, 8, 7)
    return jnp.stack((high.astype(BF16), (whole - high).astype(BF16)))


def times_unit(value, numer, denom, orient):
    re, im = value
    numer = numer % denom
    if numer == 0:
        return value
    if 8 * numer % denom == 0:
        eighth = 8 * numer // denom
        if eighth == 4:
            return -re, -im
        if eighth in (2, 6):
            return (-im, re) if (eighth == 2) == (orient > 0) else (im, -re)
    cosine = math.cos(2.0 * math.pi * numer / denom)
    sine = orient * math.sin(2.0 * math.pi * numer / denom)
    return re * cosine - im * sine, re * sine + im * cosine


def butterfly(values, orient):
    count = len(values)
    if count == 1:
        return values
    if count == 2:
        (ar, ai), (br, bi) = values
        return [(ar + br, ai + bi), (ar - br, ai - bi)]
    if count == 4:
        (ar, ai), (br, bi), (cr, ci), (dr, di) = values
        sr, si, tr, ti = ar + cr, ai + ci, ar - cr, ai - ci
        ur, ui, vr, vi = br + dr, bi + di, br - dr, bi - di
        if orient > 0:
            return [(sr + ur, si + ui), (tr - vi, ti + vr), (sr - ur, si - ui), (tr + vi, ti - vr)]
        return [(sr + ur, si + ui), (tr + vi, ti - vr), (sr - ur, si - ui), (tr - vi, ti + vr)]
    radix = 4 if count % 4 == 0 else 2
    inner = count // radix
    parts = [butterfly(values[s::radix], orient) for s in range(radix)]
    out = [None] * count
    for k in range(inner):
        joined = butterfly([times_unit(parts[s][k], s * k, count, orient) for s in range(radix)], orient)
        for part in range(radix):
            out[k + inner * part] = joined[part]
    return out


def halves(value):
    high = value.astype(BF16)
    return high, (value - high.astype(F32)).astype(BF16)


def dot(a, b, contract=((1,), (0,))):
    return lax.dot_general(a, b, (contract, ((), ())), preferred_element_type=F32)


def low_lanes(shape):
    return lax.broadcasted_iota(jnp.int32, shape, 1) < 64


def swap(value):
    return pltpu.roll(value, 64, 1)


def tile_rows(start):
    return pl.ds(pl.multiple_of(start, 8), 8)


def gather_columns(group_ref, strain_ref, out_ref):
    first = 4 * lax.rem(group_ref[0], 2)

    def piece(detector, tile, part):
        return strain_ref[pl.ds(512 * detector + first + 2 * tile + part, 64, stride=8), :]

    for tile in range(2):
        for at, (one, two) in enumerate((((0, 0), (1, 0)), ((0, 1), (1, 1)), ((2, 0), (2, 1)))):
            joined = jnp.concatenate((piece(one[0], tile, one[1]), piece(two[0], tile, two[1])), axis=0)
            out_ref[16 * tile:16 * tile + 16, 8 * at:8 * at + 8, :] = joined.T.reshape(16, 8, 128)


def prepare_templates(side_ref, *refs):
    pieces, (out_ref, norm_ref, held_ref, sems) = refs[:4], refs[4:]
    copies = []
    for at, piece in enumerate(pieces):
        copy = pltpu.make_async_copy(piece, held_ref.at[lax.rem(side_ref[0] + (4 - at), 4)], sems.at[at])
        copy.start()
        copies.append(copy)
    for copy in copies:
        copy.wait()
    total = jnp.zeros((64, 128), F32)
    for chunk in range(16):
        lanes = slice(128 * chunk, 128 * chunk + 128)
        for part in range(2):
            value = jnp.concatenate([held_ref[a, part, :, lanes] for a in range(4)], axis=0)
            total = total + value * value
            out_ref[part, lanes, :] = jnp.concatenate((value, pltpu.roll(value, 127, 1)), axis=0).T
    norm_ref[...] = jnp.sum(total.reshape(8, 8, 128), axis=0)


def first_section(in_ref, twiddle_ref, wide_ref, narrow_ref, phase_ref, out_ref, pair_ref, single_ref, turn_ref):
    lower = low_lanes((8, 128))
    for at in range(2):
        values = []
        for rank in range(RANKS):
            if at == 0:
                values.append((in_ref[rank, 0:8, :], in_ref[rank, 8:16, :]))
            else:
                one = in_ref[rank, 16:24, :]
                values.append((one, swap(one)))
        for digit, (re, im) in enumerate(butterfly(values, -1)):
            cosine, sine = twiddle_ref[0, digit:digit + 1, :], twiddle_ref[1, digit:digit + 1, :]
            re, im = re * cosine + im * sine, im * cosine - re * sine
            rows = slice(8 * digit, 8 * digit + 8)
            if at == 0:
                pair_ref[rows, 0:128] = re
                pair_ref[rows, 128:256] = im
            else:
                single_ref[rows, :] = jnp.where(lower, re, swap(im))
    high, low = halves(pair_ref[...])
    pair = dot(high, wide_ref[0]) + dot(low, wide_ref[0]) + dot(high, wide_ref[1])
    high, low = halves(single_ref[...])
    single = dot(high, narrow_ref[0]) + dot(low, narrow_ref[0]) + dot(high, narrow_ref[1])
    cosine, sine = phase_ref[0], phase_ref[1]
    re, im = pair[:, 0:128], pair[:, 128:256]
    turn_ref[0] = re * cosine - im * sine
    turn_ref[1] = im * cosine + re * sine
    turn_ref[2] = single * cosine + swap(single) * jnp.where(low_lanes((256, 128)), -sine, sine)
    for at in range(DETECTORS):
        for quad in range(2):
            blocks = []
            for part in range(2):
                source, start = (part, 64 * at) if at < 2 else (2, 64 * part)
                cols = [turn_ref[source, pl.ds(4 * quad + u, 32, stride=8), :] for u in range(4)]
                for a in range(4):
                    lanes = slice(start + 16 * a, start + 16 * a + 16)
                    blocks.append(jnp.concatenate([c[16 * h:16 * h + 16, lanes] for c in cols for h in range(2)], axis=1))
            turned = jnp.concatenate(blocks, axis=0).T
            for u in range(4):
                for h in range(2):
                    rows = pl.ds(24 * h + 8 * at + 4 * quad + u, 16, stride=48)
                    out_ref[rows, :] = turned[32 * u + 16 * h:32 * u + 16 * h + 16, :]


def slot_of(a, low):
    return 4 * (a % 2) + 2 * (low // 8) + a // 2 % 2, 16 * (low // 4 % 2) + 4 * (low % 4) + a // 4


def filter_detector(
    load, template_ref, near_ref, mix_ref, table_ref, digit_ref, fold_ref, out_ref, base, work_ref, last_ref
):
    lower = low_lanes((8, 128))

    def spread(low, carry):
        values = []
        for a in range(8):
            one = load(*slot_of(a, low))
            two = load(*slot_of(a + 8, low))
            add, sub = one + two, one - two
            re, im = jnp.where(lower, add, swap(sub)), jnp.where(lower, swap(add), sub)
            cosine, sine = fold_ref[a, 0:1, :], fold_ref[a, 1:2, :]
            values.append((re * cosine - im * sine, re * sine + im * cosine) if a else (re, im))
        for pair, (re, im) in enumerate(butterfly(values, -1)):
            cosine, sine = digit_ref[pair, 0, tile_rows(8 * low), :], digit_ref[pair, 1, tile_rows(8 * low), :]
            lanes = slice(128 * (pair % 2), 128 * (pair % 2) + 128)
            work_ref[pair // 2, tile_rows(8 * low), lanes] = re * cosine + im * sine
            work_ref[pair // 2, tile_rows(128 + 8 * low), lanes] = im * cosine - re * sine
        return carry

    lax.fori_loop(0, 16, spread, 0)

    for quad in range(4):
        high, low = halves(work_ref[quad])
        spectrum = dot(table_ref[0, 0], high) + dot(table_ref[0, 0], low) + dot(table_ref[0, 1], high)
        s_re, s_im = spectrum[0:128], spectrum[128:256]
        rows = [pl.ds(4 * quad + 2 * k, 128, stride=16) for k in range(2)]
        h_re = jnp.concatenate([template_ref[0, r, :] for r in rows], axis=1)
        h_im = jnp.concatenate([template_ref[1, r, :] for r in rows], axis=1)
        product = jnp.concatenate((s_re * h_re + s_im * h_im, s_im * h_re - s_re * h_im), axis=0)
        high, low = halves(product)
        series = dot(table_ref[1, 0], high) + dot(table_ref[1, 0], low) + dot(table_ref[1, 1], high)
        for k in range(2):
            lanes = slice(128 * k, 128 * k + 128)
            re, im = series[0:128, lanes], series[128:256, lanes]
            cosine, sine = digit_ref[2 * quad + k, 0], digit_ref[2 * quad + k, 1]
            re, im = re * cosine - im * sine, re * sine + im * cosine
            cosine, sine = near_ref[0], near_ref[1]
            work_ref[quad, 0:128, lanes] = re * cosine - im * sine
            work_ref[quad, 128:256, lanes] = re * sine + im * cosine

    def collect(step, carry):
        values = []
        for pair in range(8):
            lanes = slice(128 * (pair % 2), 128 * (pair % 2) + 128)
            rows = tile_rows(8 * step), tile_rows(128 + 8 * step)
            values.append((work_ref[pair // 2, rows[0], lanes], work_ref[pair // 2, rows[1], lanes]))
        for k, (re, im) in enumerate(butterfly(values, 1)):
            last_ref[k, tile_rows(8 * step), 0:128] = re
            last_ref[k, tile_rows(8 * step), 128:256] = im
        return carry

    lax.fori_loop(0, 16, collect, 0)
    for k in range(8):
        high, low = halves(last_ref[k])
        mixed = dot(high, mix_ref[0, k]) + dot(low, mix_ref[0, k]) + dot(high, mix_ref[1, k])
        for quarter in range(4):
            rows = slice(32 * quarter, 32 * quarter + 32)
            out_ref[4 * k + quarter, base:base + 32, :] = mixed[rows, 0:128]
            out_ref[4 * k + quarter, base + 32:base + 64, :] = mixed[rows, 128:256]


def filter_first(member_ref, *refs):
    pieces, tables, norm_ref = refs[:8], refs[8:14], refs[14]
    out_ref, work_ref, last_ref, held_ref, sems = refs[15:]
    side, core = member_ref[0], member_ref[1]
    copies = []
    for at, piece in enumerate(pieces):
        slot = 2 * lax.rem(side + (4 - at % 4), 4) + (core if at < 4 else 1 - core)
        copy = pltpu.make_async_copy(piece, held_ref.at[slot], sems.at[at])
        copy.start()
        copies.append(copy)
    for rank in range(RANKS):
        out_ref[rank, 64:72, :] = norm_ref[...]
    for copy in copies:
        copy.wait()
    filter_detector(lambda member, rank: held_ref[member, rank], *tables, out_ref, 0, work_ref, last_ref)


def filter_rest(in_ref, *refs):
    tables, (out_ref, work_ref, last_ref) = refs[:6], refs[6:]
    for at in range(2):
        filter_detector(
            lambda member, rank, rows=slice(8 * at, 8 * at + 8): in_ref[member, rank, rows, :],
            *tables, out_ref, 64 * at, work_ref, last_ref,
        )


def detector_power(in_ref, base, twiddle_ref, wide_ref, work_ref):
    def step_fn(step, carry):
        values = [
            (in_ref[r, tile_rows(base + 8 * step), :], in_ref[r, tile_rows(base + 32 + 8 * step), :])
            for r in range(RANKS)
        ]
        for digit, (re, im) in enumerate(butterfly(values, 1)):
            cosine, sine = twiddle_ref[0, digit:digit + 1, :], twiddle_ref[1, digit:digit + 1, :]
            at = 16 * (digit // 16) + 4 * (digit % 4) + digit // 4 % 4
            rows = tile_rows(32 * at + 8 * step)
            work_ref[rows, 0:128] = re * cosine - im * sine
            work_ref[rows, 128:256] = im * cosine + re * sine
        return carry

    lax.fori_loop(0, 4, step_fn, 0)

    def power_of(quad):
        high, low = halves(work_ref[pl.ds(pl.multiple_of(128 * quad, 128), 128), :])
        full = dot(high, wide_ref[0]) + dot(low, wide_ref[0]) + dot(high, wide_ref[1])
        re, im = full[:, 0:128], full[:, 128:256]
        return re * re + im * im

    return power_of


def start_power(in_ref, twiddle_ref, wide_ref, out_ref, norm_ref, work_ref):
    total = jnp.zeros((8, 128), F32)
    for rank in range(RANKS):
        total = total + in_ref[rank, 64:72, :]
    norm_ref[...] = total
    power_of = detector_power(in_ref, 0, twiddle_ref, wide_ref, work_ref)

    def step_fn(quad, carry):
        out_ref[pl.ds(pl.multiple_of(128 * quad, 128), 128), :] = power_of(quad)
        return carry

    lax.fori_loop(0, 8, step_fn, 0)


def finish_power(in_ref, twiddle_ref, wide_ref, sum_ref, norm_ref, out_ref, one_ref, two_ref):
    first = detector_power(in_ref, 0, twiddle_ref, wide_ref, one_ref)
    second = detector_power(in_ref, 64, twiddle_ref, wide_ref, two_ref)
    scale = 1.0 / (FULL * (jnp.sum(norm_ref[...]) + EPSILON))
    for quad in range(8):
        rows = slice(128 * quad, 128 * quad + 128)
        turned = ((first(quad) + second(quad) + sum_ref[rows, :]) * scale).T
        for g in range(8):
            start = 32 * (quad // 4) + 4 * (quad % 4) + 16 * (g // 4) + g % 4
            out_ref[pl.ds(start, 16, stride=64), :] = turned[16 * g:16 * g + 16, :]


def best_template(*refs):
    refs[4][...] = jnp.maximum(jnp.maximum(refs[0][...], refs[1][...]), jnp.maximum(refs[2][...], refs[3][...]))


def merge_templates(side_ref, *refs):
    one_ref, two_ref, out_ref = refs[4:]
    for block in range(8):
        rows = slice(32 * block, 32 * block + 32)
        best = jnp.maximum(one_ref[rows, :], two_ref[rows, :])
        for step in range(4):
            t = lax.rem(side_ref[0] + (4 - step), 4)
            out_ref[4 * block + t, 0:32, :] = refs[step][rows, :]
            out_ref[4 * block + t, 32:64, :] = best


def place_samples(in_ref, out_ref, best_ref):
    for k in range(8):
        for first, target in ((0, out_ref), (32, best_ref)):
            parts = [in_ref[4 * k + quarter, first:first + 32, :] for quarter in range(4)]
            for u in range(4):
                joined = jnp.concatenate([p[:, 32 * u:32 * u + 32] for p in parts], axis=1)
                for h in range(2):
                    target[pl.ds(256 * u + 8 * h + k, 16, stride=16), :] = joined[16 * h:16 * h + 16]


PARAMS = pltpu.CompilerParams(vmem_limit_bytes=VMEM_LIMIT)


def shape(*dims):
    return jax.ShapeDtypeStruct(dims, F32)


def call(kernel, out, specs, scratch=(), **kwargs):
    many = isinstance(out, (tuple, list))
    whole = pl.BlockSpec(memory_space=pltpu.VMEM)
    return pl.pallas_call(
        kernel,
        out_shape=out,
        in_specs=specs,
        out_specs=[whole] * len(out) if many else whole,
        scratch_shapes=list(scratch),
        compiler_params=PARAMS,
        **kwargs,
    )


def cost(us):
    return pl.CostEstimate(flops=int(us * 1e9), bytes_accessed=int(us * 1e6), transcendentals=0)


TIME = ("zp", "zl", "x")
BINS = ("zl", "x", "y")
ACROSS = [(0, 1), (1, 0)]


def forward(value, axis, step):
    return lax.ppermute(value, axis, [(i, (i + step) % 4) for i in range(4)]) if step else value


def gather_pieces(value, ready):
    own = [value] + [forward(value, "zp", step) for step in (1, 2, 3)]
    own, ready = lax.optimization_barrier((own, ready))
    return own + [lax.ppermute(one, "core", ACROSS) for one in own], ready


def spread_templates(masked, y):
    pieces = [lax.dynamic_index_in_dim(masked, y, 0, False)]
    for step in (1, 2, 3):
        pieces.append(forward(lax.dynamic_index_in_dim(masked, (y + step) % 4, 0, False), "y", step))
    return jnp.stack(pieces)


def move_templates(pieces, y, side, step):
    return forward(lax.dynamic_index_in_dim(pieces, (y - side - step) % 4, 0, False), "zp", step)


def local(strain, templates, pattern, cutoff):
    side, low, x, y, core = (lax.axis_index(n).astype(jnp.int32) for n in ("zp", "zl", "x", "y", "core"))
    me, group, place = 8 * side + 4 * low + x, 2 * y + core, 16 * low + 4 * x + y
    vmem = pl.BlockSpec(memory_space=pltpu.VMEM)
    smem = pl.BlockSpec(memory_space=pltpu.SMEM)
    anywhere = pl.BlockSpec(memory_space=pl.ANY)

    samples = strain.reshape(2, 3, 64, 16, 128).transpose(1, 2, 3, 0, 4).reshape(192, 32, 128)
    columns = pl.pallas_call(
        lambda group_ref, strain_ref, out_ref: gather_columns(group_ref, strain_ref.reshape(1536, 128), out_ref),
        out_shape=shape(RANKS, 24, 128),
        grid_spec=pltpu.PrefetchScalarGridSpec(
            num_scalar_prefetch=1,
            grid=(1,),
            in_specs=[pl.BlockSpec((192, 8, 128), lambda i, at: (0, at[0] // 2, 0))],
            out_specs=pl.BlockSpec((RANKS, 24, 128), lambda i, at: (0, 0, 0)),
        ),
        compiler_params=PARAMS,
        cost_estimate=cost(3),
    )(group.reshape(1), samples)
    columns = lax.all_to_all(columns, TIME, 0, 0, tiled=True)

    block_index = jnp.arange(pattern.shape[1], dtype=jnp.int32)
    active = pattern.astype(F32) * (block_index[None, :] < cutoff[:, None]).astype(F32)
    weight = jnp.repeat(active, SIDE // pattern.shape[1], axis=1)
    masked = jnp.swapaxes(templates.reshape(2, 4, 16, SIDE), 0, 1) * weight
    pieces = spread_templates(masked, y)
    pieces, group, me, place = lax.optimization_barrier((pieces, group, me, place))
    moved = [move_templates(pieces, y, side, step) for step in (0, 1, 2, 3)]

    row = jnp.arange(256, dtype=jnp.int32)[:, None]
    lane = jnp.arange(128, dtype=jnp.int32)[None, :]
    first_phase = phases((256 * group + 8 * me + row % 8) * (row // 8 + 32 * (lane % 64)), -1.0)
    columns, first_phase = lax.optimization_barrier((columns, first_phase))

    def first_bins(columns):
        rows = call(
            first_section,
            shape(RANKS * 24, 128),
            [vmem] * 5,
            [pltpu.VMEM((256, 256), F32), pltpu.VMEM((256, 128), F32), pltpu.VMEM((3, 256, 128), F32)],
            cost_estimate=cost(4),
        )(columns, jnp.asarray(row_twiddle()), jnp.asarray(first_table(2)), jnp.asarray(first_table(1)), first_phase)
        return lax.all_to_all(rows.reshape(RANKS, 24, 128), BINS, 0, 0, tiled=True)

    rows = lax.cond(place >= 0, first_bins, lambda columns: columns, columns)
    rows, moved, place = lax.optimization_barrier((rows, moved, place))
    near = phases(jnp.arange(128, dtype=jnp.int32)[:, None] * (512 * (lane // 16 % 4) + 16 * place + lane % 16), 1.0)
    mix = mixing_tables(place)
    bank, norm = call(
        prepare_templates,
        (shape(2, SIDE, 128), shape(8, 128)),
        [smem] + [anywhere] * 4,
        [pltpu.VMEM((4, 2, 16, SIDE), F32), pltpu.SemaphoreType.DMA((4,))],
        cost_estimate=cost(4),
    )(side.reshape(1), *moved)

    tables = [jnp.asarray(t) for t in (column_table(), digit_twiddle(), fold_twiddle())]
    others = lax.all_gather(rows[:, 0:16, :], ("zp", "core"), axis=0)
    pieces, (bank, near, mix) = gather_pieces(rows[:, 16:24, :], (bank, near, mix))
    tables = [near, mix] + tables
    work = [pltpu.VMEM((4, 256, 256), F32), pltpu.VMEM((8, 128, 256), F32)]
    first = call(
        filter_first,
        shape(RANKS, 72, 128),
        [smem] + [anywhere] * 8 + [vmem] * 7,
        work + [pltpu.VMEM((GROUPS, RANKS, 8, 128), F32), pltpu.SemaphoreType.DMA((8,))],
        cost_estimate=cost(8),
    )(jnp.stack((side, core)), *pieces, bank, *tables, norm)
    first = lax.all_to_all(first, BINS, 0, 0, tiled=True)
    second = call(
        filter_rest, shape(RANKS, 128, 128), [vmem] * 7, work, cost_estimate=cost(12)
    )(others, bank, *tables)
    second = lax.all_to_all(second, BINS, 0, 0, tiled=True)

    twiddle, wide = jnp.asarray(inner_twiddle()), jnp.asarray(last_table())
    work = pltpu.VMEM((1024, 256), F32)
    total, whole_norm = call(
        start_power, (shape(1024, 128), shape(8, 128)), [vmem] * 3, [work], cost_estimate=cost(3)
    )(first, twiddle, wide)
    power = call(finish_power, shape(1024, 128), [vmem] * 5, [work] * 2, cost_estimate=cost(6))(
        second, twiddle, wide, total, whole_norm
    )
    power = power.reshape(4, 256, 128)
    power = [forward(lax.dynamic_index_in_dim(power, (side + step) % 4, 0, False), "zp", step) for step in range(4)]
    best = call(best_template, shape(256, 128), [vmem] * 4, cost_estimate=cost(1))(*power)
    other = lax.ppermute(best, "core", ACROSS)
    power = call(merge_templates, shape(RANKS, 64, 128), [smem] + [vmem] * 6, cost_estimate=cost(2))(
        side.reshape(1), *power, best, other
    )
    power = lax.all_to_all(power, BINS, 0, 0, tiled=True)
    snr, peak = call(place_samples, (shape(1024, 128), shape(1024, 128)), [vmem], cost_estimate=cost(2))(power)
    return snr.reshape(1, 64 * SIDE), peak.reshape(64 * SIDE)


def solution(mesh):
    mesh = jax.sharding.Mesh(mesh.devices.reshape(4, 2, 4, 4, 2), ("zp", "zl", "x", "y", "core"))
    group = ("y", "core")
    in_specs = (P(None, None, TIME), P(None, group, TIME, None), P(group, None), P(group))
    out_specs = (P(group, TIME), P(TIME))
    return jax.shard_map(local, mesh=mesh, in_specs=in_specs, out_specs=out_specs, check_vma=False)
```

profile of v0, /device:TPU:32, one launch (start us, length us, event | category | flops | bytes accessed | tf_op | source)
XLA Modules:
  0.0 225.3 jit_solution(10996391400891610938)
XLA Ops:
  10.5 3.1 %collective-permute-start.2 = (f32[2,16,2048]{2,1,0:T(8,128)S(1)}, f32[2,16,2048]{2,1,0:T(8,128)S(1)}, u32[]{:S(2)}, u32[]{:S(2)}) collective-permute-start(f32[2,16,2048]{2,1,0:T(8,128)S(1)} %get-tuple-element.86), channel_id=1, source_target_pairs={{0,6},{2,0},{4,2},{6,4},{1,7},{3,1},{5,3},{7,5},{8,14},{10,8},{12,... | collective-permute-start | bytes 786440 | tf_op jit(solution)/shard_map/ppermute | solution.py:429
  17.8 11.2 %all-to-all-start.1 = ((f32[32,24,128]{2,1,0:T(8,128)}), f32[32,24,128]{2,1,0:T(8,128)S(1)}, u32[]{:S(2)}, u32[]{:S(2)}) async-start(f32[32,24,128]{2,1,0:T(8,128)} %shard_map.134), calls=%async_computation.1 | async-start | bytes 786432 | tf_op jit(solution)/shard_map/all_to_all | solution.py:469
  32.5 4.2 %collective-permute-start.4 = (f32[2,16,2048]{2,1,0:T(8,128)S(1)}, f32[2,16,2048]{2,1,0:T(8,128)S(1)}, u32[]{:S(2)}, u32[]{:S(2)}) collective-permute-start(f32[2,16,2048]{2,1,0:T(8,128)S(1)} %get-tuple-element.82), channel_id=1, source_target_pairs={{0,128},{64,192},{128,0},{192,64},{1,129},{65,193},{129,1},{193,65... | collective-permute-start | bytes 786440 | tf_op jit(solution)/shard_map/ppermute | solution.py:429
  36.8 2.7 %collective-permute-start.5 = (f32[2,16,2048]{2,1,0:T(8,128)S(1)}, f32[2,16,2048]{2,1,0:T(8,128)S(1)}, u32[]{:S(2)}, u32[]{:S(2)}) collective-permute-start(f32[2,16,2048]{2,1,0:T(8,128)S(1)} %get-tuple-element.81), channel_id=1, source_target_pairs={{0,192},{64,0},{128,64},{192,128},{1,193},{65,1},{129,65},{193,129... | collective-permute-start | bytes 786440 | tf_op jit(solution)/shard_map/ppermute | solution.py:429
  40.1 7.5 %all-to-all-done.1 = f32[32,24,128]{2,1,0:T(8,128)S(1)} async-done(((f32[32,24,128]{2,1,0:T(8,128)}), f32[32,24,128]{2,1,0:T(8,128)S(1)}, u32[]{:S(2)}, u32[]{:S(2)}) %all-to-all-start.1) | async-done | bytes 393248 | tf_op jit(solution)/shard_map/all_to_all | solution.py:469
  47.6 19.9 %conditional.1 = (f32[32,24,128]{2,1,0:T(8,128)S(1)}) conditional(s32[]{:T(128)} %convert_element_type.79, f32[32,24,128]{2,1,0:T(8,128)S(1)} %all-to-all-done.1, (f32[32,24,128]{2,1,0:T(8,128)S(1)}, (), (), (), f32[2,256,128]{2,1,0:T(8,128)S(1)}) %tuple.20), branch_computations={%region_0.1_spmd, %region_1.2_spmd} | conditional | flops 4000000000 | bytes 4786440 | solution.py:494
  47.6 3.1 %branch_1_fun.1 = f32[768,128]{1,0:T(8,128)} custom-call(f32[32,24,128]{2,1,0:T(8,128)S(1)} %get-tuple-element.14.in_ref, f32[2,32,128]{2,1,0:T(8,128)} %constant.329.clone.1.twiddle_ref, bf16[2,256,256]{2,1,0:T(8,128)(2,1)} %constant.330.clone.1.wide_ref, bf16[2,128,128]{2,1,0:T(8,128)(2,1)} %constant.331.clone.1.narrow_ref, ...), custom_call_target="tpu_custom_call" | custom-call | flops 4000000000 | bytes 4000000 | tf_op jit(solution)/shard_map/cond/branch_1_fun/pallas_call | solution.py:485
  50.7 16.8 %all_to_all.24 = f32[32,24,128]{2,1,0:T(8,128)S(1)} all-to-all(f32[32,24,128]{2,1,0:T(8,128)} %bitcast.56), channel_id=1, replica_groups=mesh['zp'=4,'zl'=2,'x'=4,'y'=4,'core'=2] {'zl','x','y'}, dimensions={0} | all-to-all | bytes 786432 | tf_op jit(solution)/shard_map/cond/branch_1_fun/all_to_all | solution.py:492
  69.9 3.6 %collective-permute-start.7 = (f32[32,8,128]{2,1,0:T(8,128)S(1)}, f32[32,8,128]{2,1,0:T(8,128)S(1)}, u32[]{:S(2)}, u32[]{:S(2)}) collective-permute-start(f32[32,8,128]{2,1,0:T(8,128)S(1)} %slice.7.refs_0_), channel_id=1, source_target_pairs={{0,128},{64,192},{128,0},{192,64},{1,129},{65,193},{129,1},{193,65... | collective-permute-start | bytes 393224 | tf_op jit(solution)/shard_map/ppermute | solution.py:429
  73.5 3.5 %collective-permute-start.8 = (f32[32,8,128]{2,1,0:T(8,128)S(1)}, f32[32,8,128]{2,1,0:T(8,128)S(1)}, u32[]{:S(2)}, u32[]{:S(2)}) collective-permute-start(f32[32,8,128]{2,1,0:T(8,128)S(1)} %slice.7.refs_0_), channel_id=1, source_target_pairs={{0,192},{64,0},{128,64},{192,128},{1,193},{65,1},{129,65},{193,129... | collective-permute-start | bytes 393224 | tf_op jit(solution)/shard_map/ppermute | solution.py:429
  77.9 2.4 %fusion.8 = (f32[1,8,128,128]{3,2,1,0:T(8,128)S(1)}, f32[1,8,128,128]{3,2,1,0:T(8,128)S(1)}) fusion(s32[128,128]{1,0:T(8,128)S(1)} %get-tuple-element.102, s32[128,128]{1,0:T(8,128)S(1)} %get-tuple-element.101, s32[128]{0:T(128)S(1)} %add_add_fusion, s32[8,128]{1,0:T(8,128)S(1)} %get-tuple-element.100, s32[8,128]{1,0:T(8,128)S(1)} %get-tuple-element.99, ...), kind=kLoop, calls=%fused_computation.26 | loop fusion | flops 3932160 | bytes 1188864 | tf_op jit(solution)/shard_map/cos | solution.py:73
  81.4 3.5 %shard_map.135 = (f32[2,2048,128]{2,1,0:T(8,128)}, f32[8,128]{1,0:T(8,128)}) custom-call(s32[1]{0:T(128)} %bitcast.1.side_ref, f32[2,16,2048]{2,1,0:T(8,128)} %get-tuple-element.53.refs_0_, f32[2,16,2048]{2,1,0:T(8,128)} %copy-done.3, f32[2,16,2048]{2,1,0:T(8,128)} %copy-done.4, f32[2,16,2048]{2,1,0:T(8,128)} %copy-done.5), custom_call_target="tpu_custom_call" | custom-call | flops 4000000000 | bytes 4000000 | tf_op jit(solution)/shard_map/pallas_call | solution.py:498
  89.9 9.3 %shard_map.137 = f32[32,72,128]{2,1,0:T(8,128)} custom-call(s32[2]{0:T(128)} %pad_add_fusion.member_ref, f32[32,8,128]{2,1,0:T(8,128)} %copy-done.2, f32[32,8,128]{2,1,0:T(8,128)} %copy-done.6, f32[32,8,128]{2,1,0:T(8,128)} %copy-done.7, f32[32,8,128]{2,1,0:T(8,128)} %copy-done.8, f32[32,8,128]{2,1,0:T(8,128)} %copy-done.15, f32[32,8,128]{2,1,0:T(8,128)} %copy-done.9, ...), custom_call_target="tpu_custom_call" | custom-call | flops 8000000000 | bytes 8000000 | tf_op jit(solution)/shard_map/pallas_call | solution.py:511
  99.2 6.4 %all-to-all-start.3 = ((f32[32,72,128]{2,1,0:T(8,128)}), f32[32,72,128]{2,1,0:T(8,128)S(1)}, u32[]{:S(2)}, u32[]{:S(2)}) async-start(f32[32,72,128]{2,1,0:T(8,128)} %shard_map.137), calls=%async_computation.3 | async-start | bytes 2359296 | tf_op jit(solution)/shard_map/all_to_all | solution.py:518
  105.6 4.8 %all-gather.3.cloned.1.call-done = f32[256,16,128]{2,1,0:T(8,128)} async-done(((f32[32,16,128]{2,1,0:T(8,128)}), f32[256,16,128]{2,1,0:T(8,128)}) %all-gather.3.cloned.1.call-update) | async-done | bytes 2097168 | tf_op jit(solution)/shard_map/all_gather | solution.py:507
  110.4 13.0 %shard_map.136 = f32[32,128,128]{2,1,0:T(8,128)} custom-call(f32[8,32,16,128]{3,2,1,0:T(8,128)} %bitcast.62, f32[2,2048,128]{2,1,0:T(8,128)} %get-tuple-element.59.refs_0_.refs_8_, f32[2,128,128]{2,1,0:T(8,128)} %pad_maximum_fusion.4.refs_1_.refs_9_, bf16[2,8,256,256]{3,2,1,0:T(8,128)(2,1)} %pad_maximum_fusion.1.refs_2_.refs_10_, ...), custom_call_target="tpu_custom_call" | custom-call | flops 12000000000 | bytes 12000000 | tf_op jit(solution)/shard_map/pallas_call | solution.py:519
  124.6 7.3 %all-to-all-start.2 = ((f32[32,128,128]{2,1,0:T(8,128)}), f32[32,128,128]{2,1,0:T(8,128)S(1)}, u32[]{:S(2)}, u32[]{:S(2)}) async-start(f32[32,128,128]{2,1,0:T(8,128)} %shard_map.136), calls=%async_computation.2 | async-start | bytes 4194304 | tf_op jit(solution)/shard_map/all_to_all | solution.py:522
  131.9 4.4 %shard_map.138 = (f32[1024,128]{1,0:T(8,128)}, f32[8,128]{1,0:T(8,128)}) custom-call(f32[32,72,128]{2,1,0:T(8,128)} %copy-done.1, f32[2,32,128]{2,1,0:T(8,128)} %constant.335.clone.twiddle_ref, bf16[2,256,256]{2,1,0:T(8,128)(2,1)} %constant.336.clone.wide_ref), custom_call_target="tpu_custom_call" | custom-call | flops 3000000000 | bytes 3000000 | tf_op jit(solution)/shard_map/pallas_call | solution.py:526
  136.3 23.1 %all-to-all-done.2.in_ref = f32[32,128,128]{2,1,0:T(8,128)S(1)} async-done(((f32[32,128,128]{2,1,0:T(8,128)}), f32[32,128,128]{2,1,0:T(8,128)S(1)}, u32[]{:S(2)}, u32[]{:S(2)}) %all-to-all-start.2) | async-done | bytes 2097184 | tf_op jit(solution)/shard_map/all_to_all | solution.py:522
  160.8 4.8 %shard_map.139 = f32[1024,128]{1,0:T(8,128)} custom-call(f32[32,128,128]{2,1,0:T(8,128)} %copy-done, f32[2,32,128]{2,1,0:T(8,128)} %constant.335.clone.twiddle_ref, bf16[2,256,256]{2,1,0:T(8,128)(2,1)} %constant.336.clone.wide_ref, f32[1024,128]{1,0:T(8,128)} %get-tuple-element.67.sum_ref, f32[8,128]{1,0:T(8,128)} %get-tuple-element.68.norm_ref), custom_call_target="tpu_custom_call" | custom-call | flops 6000000000 | bytes 6000000 | tf_op jit(solution)/shard_map/pallas_call | solution.py:529
  174.7 6.7 %collective-permute-done.14.refs_2_ = f32[256,128]{1,0:T(8,128)S(1)} collective-permute-done((f32[256,128]{1,0:T(8,128)S(1)}, f32[256,128]{1,0:T(8,128)S(1)}, u32[]{:S(2)}, u32[]{:S(2)}) %collective-permute-start.14) | collective-permute-done | bytes 131104 | tf_op jit(solution)/shard_map/ppermute | solution.py:429
  181.5 2.8 %collective-permute-done.15.refs_3_ = f32[256,128]{1,0:T(8,128)S(1)} collective-permute-done((f32[256,128]{1,0:T(8,128)S(1)}, f32[256,128]{1,0:T(8,128)S(1)}, u32[]{:S(2)}, u32[]{:S(2)}) %collective-permute-start.15) | collective-permute-done | bytes 131104 | tf_op jit(solution)/shard_map/ppermute | solution.py:429
  191.3 24.2 %all_to_all.25.in_ref = f32[32,64,128]{2,1,0:T(8,128)} all-to-all(f32[32,64,128]{2,1,0:T(8,128)} %shard_map.141), channel_id=1, replica_groups=mesh['zp'=4,'zl'=2,'x'=4,'y'=4,'core'=2] {'zl','x','y'}, dimensions={0} | all-to-all | bytes 2097152 | tf_op jit(solution)/shard_map/all_to_all | solution.py:539
  215.5 3.0 %shard_map.142 = (f32[1024,128]{1,0:T(8,128)}, f32[1024,128]{1,0:T(8,128)}) custom-call(f32[32,64,128]{2,1,0:T(8,128)} %all_to_all.25.in_ref), custom_call_target="tpu_custom_call" | custom-call | flops 2000000000 | bytes 2000000 | tf_op jit(solution)/shard_map/pallas_call | solution.py:540
  (97 shorter events, 38.6 us)
Async XLA Ops:
  10.5 18.8 %collective-permute-start.2 = (f32[2,16,2048]{2,1,0:T(8,128)S(1)}, f32[2,16,2048]{2,1,0:T(8,128)S(1)}, u32[]{:S(2)}, u32[]{:S(2)}) collective-permute-start(f32[2,16,2048]{2,1,0:T(8,128)S(1)} %get-tuple-element.86), channel_id=1, source_target_pairs={{0,6},{2,0},{4,2},{6,4},{1,7},{3,1},{5,3},{7,5},{8,14},{10,8},{12,... | collective-permute-start | bytes 786440 | tf_op jit(solution)/shard_map/ppermute | solution.py:429
  13.5 15.7 %collective-permute-start = (f32[2,16,2048]{2,1,0:T(8,128)S(1)}, f32[2,16,2048]{2,1,0:T(8,128)S(1)}, u32[]{:S(2)}, u32[]{:S(2)}) collective-permute-start(f32[2,16,2048]{2,1,0:T(8,128)S(1)} %get-tuple-element.88), channel_id=1, source_target_pairs={{0,2},{2,4},{4,6},{6,0},{1,3},{3,5},{5,7},{7,1},{8,10},{10,12},{12... | collective-permute-start | bytes 786440 | tf_op jit(solution)/shard_map/ppermute | solution.py:429
  13.5 15.8 %collective-permute-start.1 = (f32[2,16,2048]{2,1,0:T(8,128)S(1)}, f32[2,16,2048]{2,1,0:T(8,128)S(1)}, u32[]{:S(2)}, u32[]{:S(2)}) collective-permute-start(f32[2,16,2048]{2,1,0:T(8,128)S(1)} %get-tuple-element.87), channel_id=1, source_target_pairs={{0,4},{2,6},{4,0},{6,2},{1,5},{3,7},{5,1},{7,3},{8,12},{10,14},{12... | collective-permute-start | bytes 786440 | tf_op jit(solution)/shard_map/ppermute | solution.py:429
  17.8 29.8 %all-to-all-start.1 = ((f32[32,24,128]{2,1,0:T(8,128)}), f32[32,24,128]{2,1,0:T(8,128)S(1)}, u32[]{:S(2)}, u32[]{:S(2)}) async-start(f32[32,24,128]{2,1,0:T(8,128)} %shard_map.134), calls=%async_computation.1 | async-start | bytes 786432 | tf_op jit(solution)/shard_map/all_to_all | solution.py:469
  29.0 81.4 %all-gather.3.cloned.1.call-start = ((), (), s32[]{:S(2)}) async-start(), calls=%async_computation.5 | async-start | bytes 2359296 | tf_op jit(solution)/shard_map/all_gather | solution.py:507
  30.2 37.3 %collective-permute-start.3 = (f32[2,16,2048]{2,1,0:T(8,128)S(1)}, f32[2,16,2048]{2,1,0:T(8,128)S(1)}, u32[]{:S(2)}, u32[]{:S(2)}) collective-permute-start(f32[2,16,2048]{2,1,0:T(8,128)S(1)} %get-tuple-element.83), channel_id=1, source_target_pairs={{0,64},{64,128},{128,192},{192,0},{1,65},{65,129},{129,193},{193,1... | collective-permute-start | bytes 786440 | tf_op jit(solution)/shard_map/ppermute | solution.py:429
  32.5 34.9 %collective-permute-start.4 = (f32[2,16,2048]{2,1,0:T(8,128)S(1)}, f32[2,16,2048]{2,1,0:T(8,128)S(1)}, u32[]{:S(2)}, u32[]{:S(2)}) collective-permute-start(f32[2,16,2048]{2,1,0:T(8,128)S(1)} %get-tuple-element.82), channel_id=1, source_target_pairs={{0,128},{64,192},{128,0},{192,64},{1,129},{65,193},{129,1},{193,65... | collective-permute-start | bytes 786440 | tf_op jit(solution)/shard_map/ppermute | solution.py:429
  36.8 30.7 %collective-permute-start.5 = (f32[2,16,2048]{2,1,0:T(8,128)S(1)}, f32[2,16,2048]{2,1,0:T(8,128)S(1)}, u32[]{:S(2)}, u32[]{:S(2)}) collective-permute-start(f32[2,16,2048]{2,1,0:T(8,128)S(1)} %get-tuple-element.81), channel_id=1, source_target_pairs={{0,192},{64,0},{128,64},{192,128},{1,193},{65,1},{129,65},{193,129... | collective-permute-start | bytes 786440 | tf_op jit(solution)/shard_map/ppermute | solution.py:429
  67.4 12.9 %copy-start.3 = (f32[2,16,2048]{2,1,0:T(8,128)}, f32[2,16,2048]{2,1,0:T(8,128)S(1)}, u32[]{:S(2)}) copy-start(f32[2,16,2048]{2,1,0:T(8,128)S(1)} %collective-permute-done.3.refs_1_) | copy-start | bytes 786436
  67.5 12.9 %copy-start.4 = (f32[2,16,2048]{2,1,0:T(8,128)}, f32[2,16,2048]{2,1,0:T(8,128)S(1)}, u32[]{:S(2)}) copy-start(f32[2,16,2048]{2,1,0:T(8,128)S(1)} %collective-permute-done.4.refs_2_) | copy-start | bytes 786436
  67.5 20.3 %copy-start.2 = (f32[32,8,128]{2,1,0:T(8,128)}, f32[32,8,128]{2,1,0:T(8,128)S(1)}, u32[]{:S(2)}) copy-start(f32[32,8,128]{2,1,0:T(8,128)S(1)} %slice.7.refs_0_) | copy-start | bytes 393220
  67.5 19.6 %collective-permute-start.6 = (f32[32,8,128]{2,1,0:T(8,128)S(1)}, f32[32,8,128]{2,1,0:T(8,128)S(1)}, u32[]{:S(2)}, u32[]{:S(2)}) collective-permute-start(f32[32,8,128]{2,1,0:T(8,128)S(1)} %slice.7.refs_0_), channel_id=1, source_target_pairs={{0,64},{64,128},{128,192},{192,0},{1,65},{65,129},{129,193},{193,1... | collective-permute-start | bytes 393224 | tf_op jit(solution)/shard_map/ppermute | solution.py:429
  69.9 17.2 %collective-permute-start.7 = (f32[32,8,128]{2,1,0:T(8,128)S(1)}, f32[32,8,128]{2,1,0:T(8,128)S(1)}, u32[]{:S(2)}, u32[]{:S(2)}) collective-permute-start(f32[32,8,128]{2,1,0:T(8,128)S(1)} %slice.7.refs_0_), channel_id=1, source_target_pairs={{0,128},{64,192},{128,0},{192,64},{1,129},{65,193},{129,1},{193,65... | collective-permute-start | bytes 393224 | tf_op jit(solution)/shard_map/ppermute | solution.py:429
  73.5 13.6 %collective-permute-start.8 = (f32[32,8,128]{2,1,0:T(8,128)S(1)}, f32[32,8,128]{2,1,0:T(8,128)S(1)}, u32[]{:S(2)}, u32[]{:S(2)}) collective-permute-start(f32[32,8,128]{2,1,0:T(8,128)S(1)} %slice.7.refs_0_), channel_id=1, source_target_pairs={{0,192},{64,0},{128,64},{192,128},{1,193},{65,1},{129,65},{193,129... | collective-permute-start | bytes 393224 | tf_op jit(solution)/shard_map/ppermute | solution.py:429
  87.1 1.7 collective-permute-start.10
  87.2 1.7 collective-permute-start.11
  87.7 1.3 collective-permute-start.12
  87.8 1.4 collective-permute-start.9
  99.2 24.3 %all-to-all-start.3 = ((f32[32,72,128]{2,1,0:T(8,128)}), f32[32,72,128]{2,1,0:T(8,128)S(1)}, u32[]{:S(2)}, u32[]{:S(2)}) async-start(f32[32,72,128]{2,1,0:T(8,128)} %shard_map.137), calls=%async_computation.3 | async-start | bytes 2359296 | tf_op jit(solution)/shard_map/all_to_all | solution.py:518
  124.6 34.9 %all-to-all-start.2 = ((f32[32,128,128]{2,1,0:T(8,128)}), f32[32,128,128]{2,1,0:T(8,128)S(1)}, u32[]{:S(2)}, u32[]{:S(2)}) async-start(f32[32,128,128]{2,1,0:T(8,128)} %shard_map.136), calls=%async_computation.2 | async-start | bytes 4194304 | tf_op jit(solution)/shard_map/all_to_all | solution.py:522
  167.4 7.3 %collective-permute-start.13 = (f32[256,128]{1,0:T(8,128)S(1)}, f32[256,128]{1,0:T(8,128)S(1)}, u32[]{:S(2)}, u32[]{:S(2)}) collective-permute-start(f32[256,128]{1,0:T(8,128)S(1)} %get-tuple-element.91), channel_id=1, source_target_pairs={{0,64},{64,128},{128,192},{192,0},{1,65},{65,129},{129,193},{193,1... | collective-permute-start | bytes 393224 | tf_op jit(solution)/shard_map/ppermute | solution.py:429
  168.9 12.6 %collective-permute-start.14 = (f32[256,128]{1,0:T(8,128)S(1)}, f32[256,128]{1,0:T(8,128)S(1)}, u32[]{:S(2)}, u32[]{:S(2)}) collective-permute-start(f32[256,128]{1,0:T(8,128)S(1)} %get-tuple-element.90), channel_id=1, source_target_pairs={{0,128},{64,192},{128,0},{192,64},{1,129},{65,193},{129,1},{193,65... | collective-permute-start | bytes 393224 | tf_op jit(solution)/shard_map/ppermute | solution.py:429
  171.2 13.1 %collective-permute-start.15 = (f32[256,128]{1,0:T(8,128)S(1)}, f32[256,128]{1,0:T(8,128)S(1)}, u32[]{:S(2)}, u32[]{:S(2)}) collective-permute-start(f32[256,128]{1,0:T(8,128)S(1)} %get-tuple-element.89), channel_id=1, source_target_pairs={{0,192},{64,0},{128,64},{192,128},{1,193},{65,1},{129,65},{193,129... | collective-permute-start | bytes 393224 | tf_op jit(solution)/shard_map/ppermute | solution.py:429
  186.7 1.6 collective-permute-start.16
  (14 other events, 38.2 us)
Sparse Core Ops, SparseCore 0:
  77.9 32.4 all-gather.2
where the time goes:
time: 226 us; the launch traced here: 225 us
  starting transfers between devices  56.2 us (25%)
  waiting for transfers between devices  48.3 us (21%)
  Pallas kernels  47.2 us (21%)
  blocking collectives  41 us (18%)
  between operations  15.3 us (7%)
  other arithmetic  9.13 us (4%)
  local copies, waits for them, and re-layouts  8.3 us (4%)
    ppermute x12, starting transfers between devices, forward(): lax.ppermute(value, axis, [(i, (i + step) % 4) for i in range(4)])  30.2 us
    all_to_all x1, blocking collectives, local(): power = lax.all_to_all(power, BINS, 0, 0, tiled=True)  24.2 us
    all_to_all x1, waiting for transfers between devices, local(): second = lax.all_to_all(second, BINS, 0, 0, tiled=True)  23.1 us
    all_to_all x1, blocking collectives, first_bins(): return lax.all_to_all(rows.reshape(RANKS, 24, 128), BINS, 0, 0, tiled=True)  16.8 us
    pallas_call x1, Pallas kernels, local(): call(filter_rest, shape(RANKS, 128, 128), [vmem] * 7, work, cost_estimate...  13 us
    all_to_all x1, starting transfers between devices, local(): columns = lax.all_to_all(columns, TIME, 0, 0, tiled=True)  11.2 us
    ppermute x12, waiting for transfers between devices, forward(): lax.ppermute(value, axis, [(i, (i + step) % 4) for i in range(4)])  10.8 us
    pallas_call x1, Pallas kernels, local(): call(filter_first, shape(RANKS, 72, 128), [smem] + [anywhere] * 8 + [vmem...  9.29 us
  transfers between devices with their start and end apart: 21, of which 10 were waited for; matrix products, arithmetic and copies ran while one was open for 4% of the time, Pallas kernels for 16%

commit v1 on v0

--- a/solution.py
+++ b/solution.py
@@ -17,7 +17,7 @@
 GROUPS = 8
 F32 = jnp.float32
 BF16 = jnp.bfloat16
-VMEM_LIMIT = 56 * 1024 * 1024
+VMEM_LIMIT = 24 * 1024 * 1024
 
 
 def split_table(table):
@@ -145,6 +145,13 @@
 
 def swap(value):
     return pltpu.roll(value, 64, 1)
+
+
+def fetch(pairs, sems):
+    copies = [pltpu.make_async_copy(source, target, sems.at[at]) for at, (source, target) in enumerate(pairs)]
+    for copy in copies:
+        copy.start()
+    return copies
 
 
 def tile_rows(start):
@@ -231,7 +238,7 @@
 
 
 def filter_detector(
-    load, template_ref, near_ref, mix_ref, table_ref, digit_ref, fold_ref, out_ref, base, work_ref, last_ref
+    load, template_ref, near_ref, mix_ref, table_ref, digit_ref, fold_ref, out_ref, base, work_ref, last_ref, waits
 ):
     lower = low_lanes((8, 128))
 
@@ -251,7 +258,9 @@
             work_ref[pair // 2, tile_rows(128 + 8 * low), lanes] = im * cosine - re * sine
         return carry
 
-    lax.fori_loop(0, 16, spread, 0)
+    lax.fori_loop(0, 16, spread, 0, unroll=2)
+    for copy in waits[0]:
+        copy.wait()
 
     for quad in range(4):
         high, low = halves(work_ref[quad])
@@ -283,7 +292,9 @@
             last_ref[k, tile_rows(8 * step), 128:256] = im
         return carry
 
-    lax.fori_loop(0, 16, collect, 0)
+    lax.fori_loop(0, 16, collect, 0, unroll=2)
+    for copy in waits[1]:
+        copy.wait()
     for k in range(8):
         high, low = halves(last_ref[k])
         mixed = dot(high, mix_ref[0, k]) + dot(low, mix_ref[0, k]) + dot(high, mix_ref[1, k])
@@ -294,28 +305,39 @@
 
 
 def filter_first(member_ref, *refs):
-    pieces, tables, norm_ref = refs[:8], refs[8:14], refs[14]
-    out_ref, work_ref, last_ref, held_ref, sems = refs[15:]
+    pieces, mix_hbm, tables, norm_ref = refs[:8], refs[8], refs[9:14], refs[14]
+    out_ref, work_ref, last_ref, mix_ref, held_ref, sems = refs[15:]
     side, core = member_ref[0], member_ref[1]
-    copies = []
+    pairs = []
     for at, piece in enumerate(pieces):
         slot = 2 * lax.rem(side + (4 - at % 4), 4) + (core if at < 4 else 1 - core)
-        copy = pltpu.make_async_copy(piece, held_ref.at[slot], sems.at[at])
-        copy.start()
-        copies.append(copy)
+        pairs.append((piece, held_ref.at[slot]))
+    copies = fetch(pairs + [(mix_hbm, mix_ref)], sems)
     for rank in range(RANKS):
         out_ref[rank, 64:72, :] = norm_ref[...]
-    for copy in copies:
+    for copy in copies[:8]:
         copy.wait()
-    filter_detector(lambda member, rank: held_ref[member, rank], *tables, out_ref, 0, work_ref, last_ref)
-
-
-def filter_rest(in_ref, *refs):
-    tables, (out_ref, work_ref, last_ref) = refs[:6], refs[6:]
+    bank_ref, near_ref, table_ref, digit_ref, fold_ref = tables
+    filter_detector(
+        lambda member, rank: held_ref[member, rank],
+        bank_ref, near_ref, mix_ref, table_ref, digit_ref, fold_ref, out_ref, 0, work_ref, last_ref, ((), copies[8:]),
+    )
+
+
+def filter_rest(in_hbm, bank_hbm, near_hbm, mix_hbm, table_hbm, digit_hbm, fold_hbm, out_ref, *scratch):
+    work_ref, last_ref, bank_ref, near_ref, mix_ref, table_ref, digit_ref, fold_ref, held_ref, sems = scratch
+    pairs = [(in_hbm.at[:, :, 8 * at:8 * at + 8, :], held_ref.at[at]) for at in range(2)]
+    pairs = [pairs[0], (fold_hbm, fold_ref), (digit_hbm, digit_ref), (table_hbm, table_ref), (bank_hbm, bank_ref)] + [
+        (near_hbm, near_ref), (mix_hbm, mix_ref), pairs[1]
+    ]
+    copies = fetch(pairs, sems)
+    for copy in copies[:3]:
+        copy.wait()
     for at in range(2):
         filter_detector(
-            lambda member, rank, rows=slice(8 * at, 8 * at + 8): in_ref[member, rank, rows, :],
-            *tables, out_ref, 64 * at, work_ref, last_ref,
+            lambda member, rank, at=at: held_ref[at, member, rank],
+            bank_ref, near_ref, mix_ref, table_ref, digit_ref, fold_ref, out_ref, 64 * at, work_ref, last_ref,
+            ((), ()) if at else (copies[3:6], copies[6:8]),
         )
 
 
@@ -344,11 +366,12 @@
     return power_of
 
 
-def start_power(in_ref, twiddle_ref, wide_ref, out_ref, norm_ref, work_ref):
+def start_power(in_ref, twiddle_ref, wide_ref, out_ref, work_ref):
     total = jnp.zeros((8, 128), F32)
     for rank in range(RANKS):
         total = total + in_ref[rank, 64:72, :]
-    norm_ref[...] = total
+    out_ref[1024:1032, :] = total
+    out_ref[1032:1096, :] = twiddle_ref[...].reshape(64, 128)
     power_of = detector_power(in_ref, 0, twiddle_ref, wide_ref, work_ref)
 
     def step_fn(quad, carry):
@@ -358,10 +381,11 @@
     lax.fori_loop(0, 8, step_fn, 0)
 
 
-def finish_power(in_ref, twiddle_ref, wide_ref, sum_ref, norm_ref, out_ref, one_ref, two_ref):
+def finish_power(in_ref, wide_ref, sum_ref, out_ref, one_ref, two_ref):
+    twiddle_ref = sum_ref.at[1032:1096].reshape(2, 32, 128)
     first = detector_power(in_ref, 0, twiddle_ref, wide_ref, one_ref)
     second = detector_power(in_ref, 64, twiddle_ref, wide_ref, two_ref)
-    scale = 1.0 / (FULL * (jnp.sum(norm_ref[...]) + EPSILON))
+    scale = 1.0 / (FULL * (jnp.sum(sum_ref[1024:1032, :]) + EPSILON))
     for quad in range(8):
         rows = slice(128 * quad, 128 * quad + 128)
         turned = ((first(quad) + second(quad) + sum_ref[rows, :]) * scale).T
@@ -402,7 +426,7 @@
     return jax.ShapeDtypeStruct(dims, F32)
 
 
-def call(kernel, out, specs, scratch=(), **kwargs):
+def call(kernel, out, specs, scratch=(), limit=VMEM_LIMIT, **kwargs):
     many = isinstance(out, (tuple, list))
     whole = pl.BlockSpec(memory_space=pltpu.VMEM)
     return pl.pallas_call(
@@ -411,7 +435,7 @@
         in_specs=specs,
         out_specs=[whole] * len(out) if many else whole,
         scratch_shapes=list(scratch),
-        compiler_params=PARAMS,
+        compiler_params=pltpu.CompilerParams(vmem_limit_bytes=limit),
         **kwargs,
     )
 
@@ -479,19 +503,20 @@
     row = jnp.arange(256, dtype=jnp.int32)[:, None]
     lane = jnp.arange(128, dtype=jnp.int32)[None, :]
     first_phase = phases((256 * group + 8 * me + row % 8) * (row // 8 + 32 * (lane % 64)), -1.0)
-    columns, first_phase = lax.optimization_barrier((columns, first_phase))
-
-    def first_bins(columns):
+    fixed = [jnp.asarray(t) for t in (row_twiddle(), first_table(2), first_table(1))]
+    columns, first_phase, fixed = lax.optimization_barrier((columns, first_phase, fixed))
+
+    def first_bins(columns, first_phase, *fixed):
         rows = call(
             first_section,
             shape(RANKS * 24, 128),
             [vmem] * 5,
             [pltpu.VMEM((256, 256), F32), pltpu.VMEM((256, 128), F32), pltpu.VMEM((3, 256, 128), F32)],
             cost_estimate=cost(4),
-        )(columns, jnp.asarray(row_twiddle()), jnp.asarray(first_table(2)), jnp.asarray(first_table(1)), first_phase)
+        )(columns, *fixed, first_phase)
         return lax.all_to_all(rows.reshape(RANKS, 24, 128), BINS, 0, 0, tiled=True)
 
-    rows = lax.cond(place >= 0, first_bins, lambda columns: columns, columns)
+    rows = lax.cond(place >= 0, first_bins, lambda columns, *rest: columns, columns, first_phase, *fixed)
     rows, moved, place = lax.optimization_barrier((rows, moved, place))
     near = phases(jnp.arange(128, dtype=jnp.int32)[:, None] * (512 * (lane // 16 % 4) + 16 * place + lane % 16), 1.0)
     mix = mixing_tables(place)
@@ -504,31 +529,43 @@
     )(side.reshape(1), *moved)
 
     tables = [jnp.asarray(t) for t in (column_table(), digit_twiddle(), fold_twiddle())]
-    others = lax.all_gather(rows[:, 0:16, :], ("zp", "core"), axis=0)
-    pieces, (bank, near, mix) = gather_pieces(rows[:, 16:24, :], (bank, near, mix))
-    tables = [near, mix] + tables
+    others, early = lax.optimization_barrier((rows[:, 0:16, :], rows[:, 16:24, :]))
+    others = lax.all_gather(others, ("zp", "core"), axis=0)
+    pieces, (bank, near, mix) = gather_pieces(early, (bank, near, mix))
     work = [pltpu.VMEM((4, 256, 256), F32), pltpu.VMEM((8, 128, 256), F32)]
+    mixing = pltpu.VMEM((2, 8, 256, 256), BF16)
     first = call(
         filter_first,
         shape(RANKS, 72, 128),
-        [smem] + [anywhere] * 8 + [vmem] * 7,
-        work + [pltpu.VMEM((GROUPS, RANKS, 8, 128), F32), pltpu.SemaphoreType.DMA((8,))],
+        [smem] + [anywhere] * 9 + [vmem] * 6,
+        work + [mixing, pltpu.VMEM((GROUPS, RANKS, 8, 128), F32), pltpu.SemaphoreType.DMA((9,))],
         cost_estimate=cost(8),
-    )(jnp.stack((side, core)), *pieces, bank, *tables, norm)
+    )(jnp.stack((side, core)), *pieces, mix, bank, near, *tables, norm)
     first = lax.all_to_all(first, BINS, 0, 0, tiled=True)
     second = call(
-        filter_rest, shape(RANKS, 128, 128), [vmem] * 7, work, cost_estimate=cost(12)
-    )(others, bank, *tables)
+        filter_rest,
+        shape(RANKS, 128, 128),
+        [anywhere] * 7,
+        work
+        + [
+            pltpu.VMEM((2, SIDE, 128), F32),
+            pltpu.VMEM((2, 128, 128), F32),
+            mixing,
+            pltpu.VMEM((2, 2, 256, 256), BF16),
+            pltpu.VMEM((8, 2, 128, 128), F32),
+            pltpu.VMEM((8, 2, 128), F32),
+            pltpu.VMEM((2, GROUPS, RANKS, 8, 128), F32),
+            pltpu.SemaphoreType.DMA((8,)),
+        ],
+        limit=58 * 1024 * 1024,
+        cost_estimate=cost(12),
+    )(others, bank, near, mix, *tables)
     second = lax.all_to_all(second, BINS, 0, 0, tiled=True)
 
     twiddle, wide = jnp.asarray(inner_twiddle()), jnp.asarray(last_table())
     work = pltpu.VMEM((1024, 256), F32)
-    total, whole_norm = call(
-        start_power, (shape(1024, 128), shape(8, 128)), [vmem] * 3, [work], cost_estimate=cost(3)
-    )(first, twiddle, wide)
-    power = call(finish_power, shape(1024, 128), [vmem] * 5, [work] * 2, cost_estimate=cost(6))(
-        second, twiddle, wide, total, whole_norm
-    )
+    total = call(start_power, shape(1096, 128), [vmem] * 3, [work], cost_estimate=cost(3))(first, twiddle, wide)
+    power = call(finish_power, shape(1024, 128), [vmem] * 3, [work] * 2, cost_estimate=cost(6))(second, wide, total)
     power = power.reshape(4, 256, 128)
     power = [forward(lax.dynamic_index_in_dim(power, (side + step) % 4, 0, False), "zp", step) for step in range(4)]
     best = call(best_template, shape(256, 128), [vmem] * 4, cost_estimate=cost(1))(*power)

time: 226 us -> 216 us (0.956)
  Pallas kernels: 47.2 us -> 26.4 us
  blocking collectives: 41 us -> 47.7 us
  starting transfers between devices: 56.2 us -> 60.1 us
  waiting for transfers between devices: 48.3 us -> 50.6 us
    pallas_call x4, Pallas kernels: 31.5 us -> 21 us  [the longest x1 9.88 us: local(): call(filter_rest, shape(RANKS, 128, 128), [anywhere] * 7, work + [pltpu.V...]
    all_gather x1, waiting for transfers between devices: 4.8 us -> 13.9 us  [local(): others = lax.all_gather(others, ('zp', 'core'), axis=0)]
    all_to_all x1, waiting for transfers between devices: 7.5 us -> 0.01 us  [local(): columns = lax.all_to_all(columns, TIME, 0, 0, tiled=True)]
    all_to_all x1, blocking collectives: 16.8 us -> 23.3 us  [first_bins(): return lax.all_to_all(rows.reshape(RANKS, 24, 128), BINS, 0, 0, tiled=True)]
    pallas_call x1, Pallas kernels: 3.5 us -> 1.05 us  [local(): call(prepare_templates, (shape(2, SIDE, 128), shape(8, 128)), [smem] + [a...]
  transfers between devices with their start and end apart: 21 -> 21, of which waited for: 10 -> 12; matrix products, arithmetic and copies ran while one was open for 4% -> 3% of each run, Pallas kernels for 16% -> 10%
where the time goes in v1:
time: 216 us; the launch traced here: 215 us
  starting transfers between devices  60.1 us (28%)
  waiting for transfers between devices  50.6 us (23%)
  blocking collectives  47.7 us (22%)
  Pallas kernels  26.4 us (12%)
  between operations  15.3 us (7%)
  other arithmetic  8.82 us (4%)
  local copies, waits for them, and re-layouts  6.17 us (3%)
    ppermute x12, starting transfers between devices, forward(): lax.ppermute(value, axis, [(i, (i + step) % 4) for i in range(4)])  31 us
    all_to_all x1, blocking collectives, local(): power = lax.all_to_all(power, BINS, 0, 0, tiled=True)  24.4 us
    all_to_all x1, waiting for transfers between devices, local(): second = lax.all_to_all(second, BINS, 0, 0, tiled=True)  23.7 us
    all_to_all x1, blocking collectives, first_bins(): return lax.all_to_all(rows.reshape(RANKS, 24, 128), BINS, 0, 0, tiled=True)  23.3 us
    all_gather x1, waiting for transfers between devices, local(): others = lax.all_gather(others, ('zp', 'core'), axis=0)  13.9 us
    all_to_all x1, starting transfers between devices, local(): columns = lax.all_to_all(columns, TIME, 0, 0, tiled=True)  11.2 us
    ppermute x12, waiting for transfers between devices, forward(): lax.ppermute(value, axis, [(i, (i + step) % 4) for i in range(4)])  10.7 us
    pallas_call x1, Pallas kernels, local(): call(filter_rest, shape(RANKS, 128, 128), [anywhere] * 7, work + [pltpu.V...  9.88 us
  transfers between devices with their start and end apart: 21, of which 12 were waited for; matrix products, arithmetic and copies ran while one was open for 3% of the time, Pallas kernels for 10%

profile of v1, /device:TPU:32, one launch (start us, length us, event | category | flops | bytes accessed | tf_op | source)
XLA Modules:
  0.0 215.1 jit_solution(2004369490835895894)
XLA Ops:
  9.0 2.5 %broadcast_multiply_fusion = f32[2,4,16,2048]{3,2,1,0:T(8,128)} fusion(f32[2,4,16,2048]{3,2,1,0:T(8,128)} %bitcast.57, f32[2048]{0:T(1024)S(1)} %broadcast_in_dim.5), kind=kLoop, calls=%fused_computation.23 | loop fusion | flops 262144 | bytes 2105344 | tf_op jit(solution)/shard_map/mul | solution.py:498
  13.6 3.0 %collective-permute-start.2 = (f32[2,16,2048]{2,1,0:T(8,128)}, f32[2,16,2048]{2,1,0:T(8,128)}, u32[]{:S(2)}, u32[]{:S(2)}) collective-permute-start(f32[2,16,2048]{2,1,0:T(8,128)} %get-tuple-element.86), channel_id=1, source_target_pairs={{0,6},{2,0},{4,2},{6,4},{1,7},{3,1},{5,3},{7,5},{8,14},{10,8},{12,... | collective-permute-start | bytes 786440 | tf_op jit(solution)/shard_map/ppermute | solution.py:453
  19.2 11.2 %all-to-all-start.1 = ((f32[32,24,128]{2,1,0:T(8,128)}), f32[32,24,128]{2,1,0:T(8,128)S(1)}, u32[]{:S(2)}, u32[]{:S(2)}) async-start(f32[32,24,128]{2,1,0:T(8,128)} %shard_map.131), calls=%async_computation.1 | async-start | bytes 786432 | tf_op jit(solution)/shard_map/all_to_all | solution.py:493
  33.2 3.3 %collective-permute-start.3 = (f32[2,16,2048]{2,1,0:T(8,128)S(1)}, f32[2,16,2048]{2,1,0:T(8,128)S(1)}, u32[]{:S(2)}, u32[]{:S(2)}) collective-permute-start(f32[2,16,2048]{2,1,0:T(8,128)S(1)} %get-tuple-element.83), channel_id=1, source_target_pairs={{0,64},{64,128},{128,192},{192,0},{1,65},{65,129},{129,193},{193,1... | collective-permute-start | bytes 786440 | tf_op jit(solution)/shard_map/ppermute | solution.py:453
  36.5 4.5 %collective-permute-start.4 = (f32[2,16,2048]{2,1,0:T(8,128)S(1)}, f32[2,16,2048]{2,1,0:T(8,128)S(1)}, u32[]{:S(2)}, u32[]{:S(2)}) collective-permute-start(f32[2,16,2048]{2,1,0:T(8,128)S(1)} %get-tuple-element.82), channel_id=1, source_target_pairs={{0,128},{64,192},{128,0},{192,64},{1,129},{65,193},{129,1},{193,65... | collective-permute-start | bytes 786440 | tf_op jit(solution)/shard_map/ppermute | solution.py:453
  41.0 2.7 %collective-permute-start.5 = (f32[2,16,2048]{2,1,0:T(8,128)S(1)}, f32[2,16,2048]{2,1,0:T(8,128)S(1)}, u32[]{:S(2)}, u32[]{:S(2)}) collective-permute-start(f32[2,16,2048]{2,1,0:T(8,128)S(1)} %get-tuple-element.81), channel_id=1, source_target_pairs={{0,192},{64,0},{128,64},{192,128},{1,193},{65,1},{129,65},{193,129... | collective-permute-start | bytes 786440 | tf_op jit(solution)/shard_map/ppermute | solution.py:453
  44.4 24.8 %conditional.1 = (f32[32,24,128]{2,1,0:T(8,128)S(1)}) conditional(s32[]{:T(128)} %convert_element_type.79, f32[32,24,128]{2,1,0:T(8,128)S(1)} %all-to-all-done.1, (f32[32,24,128]{2,1,0:T(8,128)S(1)}, f32[2,32,128]{2,1,0:T(8,128)S(1)}, bf16[2,256,256]{2,1,0:T(8,128)(2,1)S(1)}, bf16[2,128,128]{2,1,0:T(8,128)(2,1)S(1)}, ...), branch_computations={%region_0.1_spmd, %region_1.2_spmd} | conditional | flops 4000000000 | bytes 4786440 | solution.py:519
  45.8 23.3 %all_to_all.24 = f32[32,24,128]{2,1,0:T(8,128)S(1)} all-to-all(f32[32,24,128]{2,1,0:T(8,128)S(1)} %bitcast.55), channel_id=1, replica_groups=mesh['zp'=4,'zl'=2,'x'=4,'y'=4,'core'=2] {'zl','x','y'}, dimensions={0} | all-to-all | bytes 786432 | tf_op jit(solution)/shard_map/cond/branch_1_fun/all_to_all | solution.py:517
  69.9 2.4 %collective-permute-start.6 = (f32[32,8,128]{2,1,0:T(8,128)S(1)}, f32[32,8,128]{2,1,0:T(8,128)S(1)}, u32[]{:S(2)}, u32[]{:S(2)}) collective-permute-start(f32[32,8,128]{2,1,0:T(8,128)S(1)} %slice.7.refs_0_), channel_id=1, source_target_pairs={{0,64},{64,128},{128,192},{192,0},{1,65},{65,129},{129,193},{193,1... | collective-permute-start | bytes 393224 | tf_op jit(solution)/shard_map/ppermute | solution.py:453
  72.3 3.6 %collective-permute-start.7 = (f32[32,8,128]{2,1,0:T(8,128)S(1)}, f32[32,8,128]{2,1,0:T(8,128)S(1)}, u32[]{:S(2)}, u32[]{:S(2)}) collective-permute-start(f32[32,8,128]{2,1,0:T(8,128)S(1)} %slice.7.refs_0_), channel_id=1, source_target_pairs={{0,128},{64,192},{128,0},{192,64},{1,129},{65,193},{129,1},{193,65... | collective-permute-start | bytes 393224 | tf_op jit(solution)/shard_map/ppermute | solution.py:453
  75.9 3.5 %collective-permute-start.8 = (f32[32,8,128]{2,1,0:T(8,128)S(1)}, f32[32,8,128]{2,1,0:T(8,128)S(1)}, u32[]{:S(2)}, u32[]{:S(2)}) collective-permute-start(f32[32,8,128]{2,1,0:T(8,128)S(1)} %slice.7.refs_0_), channel_id=1, source_target_pairs={{0,192},{64,0},{128,64},{192,128},{1,193},{65,1},{129,65},{193,129... | collective-permute-start | bytes 393224 | tf_op jit(solution)/shard_map/ppermute | solution.py:453
  79.6 2.4 %fusion.8 = (f32[1,8,128,128]{3,2,1,0:T(8,128)S(1)}, f32[1,8,128,128]{3,2,1,0:T(8,128)S(1)}) fusion(s32[128,128]{1,0:T(8,128)S(1)} %get-tuple-element.102, s32[128,128]{1,0:T(8,128)S(1)} %get-tuple-element.101, s32[128]{0:T(128)S(1)} %add_add_fusion, s32[8,128]{1,0:T(8,128)S(1)} %get-tuple-element.100, s32[8,128]{1,0:T(8,128)S(1)} %get-tuple-element.99, ...), kind=kLoop, calls=%fused_computation.26 | loop fusion | flops 3932160 | bytes 1188864 | tf_op jit(solution)/shard_map/cos | solution.py:73
  86.6 6.6 %shard_map.134 = f32[32,72,128]{2,1,0:T(8,128)} custom-call(s32[2]{0:T(128)S(1)} %pad_add_fusion.member_ref, f32[32,8,128]{2,1,0:T(8,128)S(1)} %slice.7.refs_0_, f32[32,8,128]{2,1,0:T(8,128)S(1)} %collective-permute-done.6.refs_1_, f32[32,8,128]{2,1,0:T(8,128)S(1)} %collective-permute-done.7.refs_2_, f32[32,8,128]{2,1,0:T(8,128)S(1)} %collective-permute-done.8.refs_3_, ...), custom_call_target="tpu_custom_call" | custom-call | flops 8000000000 | bytes 8000000 | tf_op jit(solution)/shard_map/pallas_call | solution.py:537
  93.2 8.3 %all-to-all-start.3 = ((f32[32,72,128]{2,1,0:T(8,128)}), f32[32,72,128]{2,1,0:T(8,128)S(1)}, u32[]{:S(2)}, u32[]{:S(2)}) async-start(f32[32,72,128]{2,1,0:T(8,128)} %shard_map.134), calls=%async_computation.3 | async-start | bytes 2359296 | tf_op jit(solution)/shard_map/all_to_all | solution.py:544
  101.5 13.9 %all-gather.3.cloned.1.call-done = f32[256,16,128]{2,1,0:T(8,128)} async-done(((f32[32,16,128]{2,1,0:T(8,128)}), f32[256,16,128]{2,1,0:T(8,128)}) %all-gather.3.cloned.1.call-update) | async-done | bytes 2097168 | tf_op jit(solution)/shard_map/all_gather | solution.py:533
  115.4 9.9 %shard_map.133 = f32[32,128,128]{2,1,0:T(8,128)} custom-call(f32[8,32,16,128]{3,2,1,0:T(8,128)} %bitcast.59, f32[2,2048,128]{2,1,0:T(8,128)} %copy-done.8, f32[2,128,128]{2,1,0:T(8,128)} %copy-done.1, bf16[2,8,256,256]{3,2,1,0:T(8,128)(2,1)} %copy-done, bf16[2,2,256,256]{3,2,1,0:T(8,128)(2,1)} %constant.332.clone.table_hbm.refs_11_, ...), custom_call_target="tpu_custom_call" | custom-call | flops 12000000000 | bytes 12000000 | tf_op jit(solution)/shard_map/pallas_call | solution.py:545
  125.3 8.4 %all-to-all-start.2 = ((f32[32,128,128]{2,1,0:T(8,128)}), f32[32,128,128]{2,1,0:T(8,128)S(1)}, u32[]{:S(2)}, u32[]{:S(2)}) async-start(f32[32,128,128]{2,1,0:T(8,128)} %shard_map.133), calls=%async_computation.2 | async-start | bytes 4194304 | tf_op jit(solution)/shard_map/all_to_all | solution.py:563
  134.5 2.2 %shard_map.135.sum_ref = f32[1096,128]{1,0:T(8,128)S(1)} custom-call(f32[32,72,128]{2,1,0:T(8,128)S(1)} %all-to-all-done.3.in_ref, f32[2,32,128]{2,1,0:T(8,128)S(1)} %copy-done.6, bf16[2,256,256]{2,1,0:T(8,128)(2,1)S(1)} %copy-done.5), custom_call_target="tpu_custom_call" | custom-call | flops 3000000000 | bytes 3000000 | tf_op jit(solution)/shard_map/pallas_call | solution.py:567
  137.6 23.7 %all-to-all-done.2.in_ref = f32[32,128,128]{2,1,0:T(8,128)S(1)} async-done(((f32[32,128,128]{2,1,0:T(8,128)}), f32[32,128,128]{2,1,0:T(8,128)S(1)}, u32[]{:S(2)}, u32[]{:S(2)}) %all-to-all-start.2) | async-done | bytes 2097184 | tf_op jit(solution)/shard_map/all_to_all | solution.py:563
  162.4 2.2 %shard_map.136 = f32[1024,128]{1,0:T(8,128)S(1)} custom-call(f32[32,128,128]{2,1,0:T(8,128)S(1)} %all-to-all-done.2.in_ref, bf16[2,256,256]{2,1,0:T(8,128)(2,1)S(1)} %copy-done.5, f32[1096,128]{1,0:T(8,128)S(1)} %copy-done.10), custom_call_target="tpu_custom_call" | custom-call | flops 6000000000 | bytes 6000000 | tf_op jit(solution)/shard_map/pallas_call | solution.py:568
  165.5 3.5 %collective-permute-start.14 = (f32[256,128]{1,0:T(8,128)S(1)}, f32[256,128]{1,0:T(8,128)S(1)}, u32[]{:S(2)}, u32[]{:S(2)}) collective-permute-start(f32[256,128]{1,0:T(8,128)S(1)} %get-tuple-element.90), channel_id=1, source_target_pairs={{0,128},{64,192},{128,0},{192,64},{1,129},{65,193},{129,1},{193,65... | collective-permute-start | bytes 393224 | tf_op jit(solution)/shard_map/ppermute | solution.py:453
  173.1 4.9 %collective-permute-done.14.refs_2_ = f32[256,128]{1,0:T(8,128)S(1)} collective-permute-done((f32[256,128]{1,0:T(8,128)S(1)}, f32[256,128]{1,0:T(8,128)S(1)}, u32[]{:S(2)}, u32[]{:S(2)}) %collective-permute-start.14) | collective-permute-done | bytes 131104 | tf_op jit(solution)/shard_map/ppermute | solution.py:453
  178.1 2.4 %collective-permute-done.15.refs_3_ = f32[256,128]{1,0:T(8,128)S(1)} collective-permute-done((f32[256,128]{1,0:T(8,128)S(1)}, f32[256,128]{1,0:T(8,128)S(1)}, u32[]{:S(2)}, u32[]{:S(2)}) %collective-permute-start.15) | collective-permute-done | bytes 131104 | tf_op jit(solution)/shard_map/ppermute | solution.py:453
  182.1 24.4 %all_to_all.25.in_ref = f32[32,64,128]{2,1,0:T(8,128)S(1)} all-to-all(f32[32,64,128]{2,1,0:T(8,128)S(1)} %shard_map.138), channel_id=1, replica_groups=mesh['zp'=4,'zl'=2,'x'=4,'y'=4,'core'=2] {'zl','x','y'}, dimensions={0} | all-to-all | bytes 2097152 | tf_op jit(solution)/shard_map/all_to_all | solution.py:576
  (91 shorter events, 26.8 us)
Async XLA Ops:
  13.6 17.1 %collective-permute-start.2 = (f32[2,16,2048]{2,1,0:T(8,128)}, f32[2,16,2048]{2,1,0:T(8,128)}, u32[]{:S(2)}, u32[]{:S(2)}) collective-permute-start(f32[2,16,2048]{2,1,0:T(8,128)} %get-tuple-element.86), channel_id=1, source_target_pairs={{0,6},{2,0},{4,2},{6,4},{1,7},{3,1},{5,3},{7,5},{8,14},{10,8},{12,... | collective-permute-start | bytes 786440 | tf_op jit(solution)/shard_map/ppermute | solution.py:453
  16.6 14.1 %collective-permute-start.1 = (f32[2,16,2048]{2,1,0:T(8,128)}, f32[2,16,2048]{2,1,0:T(8,128)}, u32[]{:S(2)}, u32[]{:S(2)}) collective-permute-start(f32[2,16,2048]{2,1,0:T(8,128)} %get-tuple-element.87), channel_id=1, source_target_pairs={{0,4},{2,6},{4,0},{6,2},{1,5},{3,7},{5,1},{7,3},{8,12},{10,14},{12... | collective-permute-start | bytes 786440 | tf_op jit(solution)/shard_map/ppermute | solution.py:453
  17.2 14.6 %collective-permute-start = (f32[2,16,2048]{2,1,0:T(8,128)}, f32[2,16,2048]{2,1,0:T(8,128)}, u32[]{:S(2)}, u32[]{:S(2)}) collective-permute-start(f32[2,16,2048]{2,1,0:T(8,128)} %get-tuple-element.88), channel_id=1, source_target_pairs={{0,2},{2,4},{4,6},{6,0},{1,3},{3,5},{5,7},{7,1},{8,10},{10,12},{12... | collective-permute-start | bytes 786440 | tf_op jit(solution)/shard_map/ppermute | solution.py:453
  19.2 25.1 %all-to-all-start.1 = ((f32[32,24,128]{2,1,0:T(8,128)}), f32[32,24,128]{2,1,0:T(8,128)S(1)}, u32[]{:S(2)}, u32[]{:S(2)}) async-start(f32[32,24,128]{2,1,0:T(8,128)} %shard_map.131), calls=%async_computation.1 | async-start | bytes 786432 | tf_op jit(solution)/shard_map/all_to_all | solution.py:493
  30.4 85.0 %all-gather.3.cloned.1.call-start = ((), (), s32[]{:S(2)}) async-start(), calls=%async_computation.5 | async-start | bytes 2359296 | tf_op jit(solution)/shard_map/all_gather | solution.py:533
  31.8 12.5 %copy-start.11 = (bf16[2,256,256]{2,1,0:T(8,128)(2,1)S(1)}, bf16[2,256,256]{2,1,0:T(8,128)(2,1)}, u32[]{:S(2)}) copy-start(bf16[2,256,256]{2,1,0:T(8,128)(2,1)} %constant.330.clone) | copy-start | bytes 786436
  31.8 12.5 %copy-start.12 = (bf16[2,128,128]{2,1,0:T(8,128)(2,1)S(1)}, bf16[2,128,128]{2,1,0:T(8,128)(2,1)}, u32[]{:S(2)}) copy-start(bf16[2,128,128]{2,1,0:T(8,128)(2,1)} %constant.331.clone) | copy-start | bytes 196612
  31.8 12.5 %copy-start.13 = (f32[2,32,128]{2,1,0:T(8,128)S(1)}, f32[2,32,128]{2,1,0:T(8,128)}, u32[]{:S(2)}) copy-start(f32[2,32,128]{2,1,0:T(8,128)} %constant.329.clone) | copy-start | bytes 98308
  33.2 36.0 %collective-permute-start.3 = (f32[2,16,2048]{2,1,0:T(8,128)S(1)}, f32[2,16,2048]{2,1,0:T(8,128)S(1)}, u32[]{:S(2)}, u32[]{:S(2)}) collective-permute-start(f32[2,16,2048]{2,1,0:T(8,128)S(1)} %get-tuple-element.83), channel_id=1, source_target_pairs={{0,64},{64,128},{128,192},{192,0},{1,65},{65,129},{129,193},{193,1... | collective-permute-start | bytes 786440 | tf_op jit(solution)/shard_map/ppermute | solution.py:453
  36.5 32.6 %collective-permute-start.4 = (f32[2,16,2048]{2,1,0:T(8,128)S(1)}, f32[2,16,2048]{2,1,0:T(8,128)S(1)}, u32[]{:S(2)}, u32[]{:S(2)}) collective-permute-start(f32[2,16,2048]{2,1,0:T(8,128)S(1)} %get-tuple-element.82), channel_id=1, source_target_pairs={{0,128},{64,192},{128,0},{192,64},{1,129},{65,193},{129,1},{193,65... | collective-permute-start | bytes 786440 | tf_op jit(solution)/shard_map/ppermute | solution.py:453
  41.0 28.1 %collective-permute-start.5 = (f32[2,16,2048]{2,1,0:T(8,128)S(1)}, f32[2,16,2048]{2,1,0:T(8,128)S(1)}, u32[]{:S(2)}, u32[]{:S(2)}) collective-permute-start(f32[2,16,2048]{2,1,0:T(8,128)S(1)} %get-tuple-element.81), channel_id=1, source_target_pairs={{0,192},{64,0},{128,64},{192,128},{1,193},{65,1},{129,65},{193,129... | collective-permute-start | bytes 786440 | tf_op jit(solution)/shard_map/ppermute | solution.py:453
  69.9 14.4 %collective-permute-start.6 = (f32[32,8,128]{2,1,0:T(8,128)S(1)}, f32[32,8,128]{2,1,0:T(8,128)S(1)}, u32[]{:S(2)}, u32[]{:S(2)}) collective-permute-start(f32[32,8,128]{2,1,0:T(8,128)S(1)} %slice.7.refs_0_), channel_id=1, source_target_pairs={{0,64},{64,128},{128,192},{192,0},{1,65},{65,129},{129,193},{193,1... | collective-permute-start | bytes 393224 | tf_op jit(solution)/shard_map/ppermute | solution.py:453
  72.3 12.1 %collective-permute-start.7 = (f32[32,8,128]{2,1,0:T(8,128)S(1)}, f32[32,8,128]{2,1,0:T(8,128)S(1)}, u32[]{:S(2)}, u32[]{:S(2)}) collective-permute-start(f32[32,8,128]{2,1,0:T(8,128)S(1)} %slice.7.refs_0_), channel_id=1, source_target_pairs={{0,128},{64,192},{128,0},{192,64},{1,129},{65,193},{129,1},{193,65... | collective-permute-start | bytes 393224 | tf_op jit(solution)/shard_map/ppermute | solution.py:453
  75.9 8.6 %collective-permute-start.8 = (f32[32,8,128]{2,1,0:T(8,128)S(1)}, f32[32,8,128]{2,1,0:T(8,128)S(1)}, u32[]{:S(2)}, u32[]{:S(2)}) collective-permute-start(f32[32,8,128]{2,1,0:T(8,128)S(1)} %slice.7.refs_0_), channel_id=1, source_target_pairs={{0,192},{64,0},{128,64},{192,128},{1,193},{65,1},{129,65},{193,129... | collective-permute-start | bytes 393224 | tf_op jit(solution)/shard_map/ppermute | solution.py:453
  84.5 1.3 collective-permute-start.9
  84.5 1.5 collective-permute-start.10
  85.0 1.3 collective-permute-start.11
  85.0 1.5 collective-permute-start.12
  93.2 32.1 %all-to-all-start.3 = ((f32[32,72,128]{2,1,0:T(8,128)}), f32[32,72,128]{2,1,0:T(8,128)S(1)}, u32[]{:S(2)}, u32[]{:S(2)}) async-start(f32[32,72,128]{2,1,0:T(8,128)} %shard_map.134), calls=%async_computation.3 | async-start | bytes 2359296 | tf_op jit(solution)/shard_map/all_to_all | solution.py:544
  125.3 36.0 %all-to-all-start.2 = ((f32[32,128,128]{2,1,0:T(8,128)}), f32[32,128,128]{2,1,0:T(8,128)S(1)}, u32[]{:S(2)}, u32[]{:S(2)}) async-start(f32[32,128,128]{2,1,0:T(8,128)} %shard_map.133), calls=%async_computation.2 | async-start | bytes 4194304 | tf_op jit(solution)/shard_map/all_to_all | solution.py:563
  164.7 8.5 %collective-permute-start.13 = (f32[256,128]{1,0:T(8,128)S(1)}, f32[256,128]{1,0:T(8,128)S(1)}, u32[]{:S(2)}, u32[]{:S(2)}) collective-permute-start(f32[256,128]{1,0:T(8,128)S(1)} %get-tuple-element.91), channel_id=1, source_target_pairs={{0,64},{64,128},{128,192},{192,0},{1,65},{65,129},{129,193},{193,1... | collective-permute-start | bytes 393224 | tf_op jit(solution)/shard_map/ppermute | solution.py:453
  165.5 12.6 %collective-permute-start.14 = (f32[256,128]{1,0:T(8,128)S(1)}, f32[256,128]{1,0:T(8,128)S(1)}, u32[]{:S(2)}, u32[]{:S(2)}) collective-permute-start(f32[256,128]{1,0:T(8,128)S(1)} %get-tuple-element.90), channel_id=1, source_target_pairs={{0,128},{64,192},{128,0},{192,64},{1,129},{65,193},{129,1},{193,65... | collective-permute-start | bytes 393224 | tf_op jit(solution)/shard_map/ppermute | solution.py:453
  169.0 11.5 %collective-permute-start.15 = (f32[256,128]{1,0:T(8,128)S(1)}, f32[256,128]{1,0:T(8,128)S(1)}, u32[]{:S(2)}, u32[]{:S(2)}) collective-permute-start(f32[256,128]{1,0:T(8,128)S(1)} %get-tuple-element.89), channel_id=1, source_target_pairs={{0,192},{64,0},{128,64},{192,128},{1,193},{65,1},{129,65},{193,129... | collective-permute-start | bytes 393224 | tf_op jit(solution)/shard_map/ppermute | solution.py:453
  180.5 1.4 collective-permute-start.16
  (11 other events, 48.1 us)
Sparse Core Ops, SparseCore 0:
  79.6 35.7 all-gather.2

commit v2 on v1

--- a/solution.py
+++ b/solution.py
@@ -305,22 +305,23 @@
 
 
 def filter_first(member_ref, *refs):
-    pieces, mix_hbm, tables, norm_ref = refs[:8], refs[8], refs[9:14], refs[14]
-    out_ref, work_ref, last_ref, mix_ref, held_ref, sems = refs[15:]
+    pieces, mix_hbm, tables, norm_ref = refs[:10], refs[10], refs[11:16], refs[16]
+    out_ref, work_ref, last_ref, mix_ref, held_ref, sems = refs[17:]
     side, core = member_ref[0], member_ref[1]
     pairs = []
     for at, piece in enumerate(pieces):
-        slot = 2 * lax.rem(side + (4 - at % 4), 4) + (core if at < 4 else 1 - core)
-        pairs.append((piece, held_ref.at[slot]))
+        step, first = ((0, 0), (3, 0), (1, 0), (2, 0), (2, 16))[at % 5]
+        slot = 2 * lax.rem(side + step, 4) + (core if at < 5 else 1 - core)
+        pairs.append((piece, held_ref.at[slot, pl.ds(first, piece.shape[0])]))
     copies = fetch(pairs + [(mix_hbm, mix_ref)], sems)
     for rank in range(RANKS):
         out_ref[rank, 64:72, :] = norm_ref[...]
-    for copy in copies[:8]:
+    for copy in copies[:10]:
         copy.wait()
     bank_ref, near_ref, table_ref, digit_ref, fold_ref = tables
     filter_detector(
         lambda member, rank: held_ref[member, rank],
-        bank_ref, near_ref, mix_ref, table_ref, digit_ref, fold_ref, out_ref, 0, work_ref, last_ref, ((), copies[8:]),
+        bank_ref, near_ref, mix_ref, table_ref, digit_ref, fold_ref, out_ref, 0, work_ref, last_ref, ((), copies[10:]),
     )
 
 
@@ -419,9 +420,6 @@
                     target[pl.ds(256 * u + 8 * h + k, 16, stride=16), :] = joined[16 * h:16 * h + 16]
 
 
-PARAMS = pltpu.CompilerParams(vmem_limit_bytes=VMEM_LIMIT)
-
-
 def shape(*dims):
     return jax.ShapeDtypeStruct(dims, F32)
 
@@ -454,7 +452,9 @@
 
 
 def gather_pieces(value, ready):
-    own = [value] + [forward(value, "zp", step) for step in (1, 2, 3)]
+    half = value.shape[0] // 2
+    back, ahead = forward(value, "zp", 1), forward(value, "zp", 3)
+    own = [value, back, ahead, forward(back[:half], "zp", 1), forward(ahead[half:], "zp", 3)]
     own, ready = lax.optimization_barrier((own, ready))
     return own + [lax.ppermute(one, "core", ACROSS) for one in own], ready
 
@@ -487,9 +487,10 @@
             in_specs=[pl.BlockSpec((192, 8, 128), lambda i, at: (0, at[0] // 2, 0))],
             out_specs=pl.BlockSpec((RANKS, 24, 128), lambda i, at: (0, 0, 0)),
         ),
-        compiler_params=PARAMS,
+        compiler_params=pltpu.CompilerParams(vmem_limit_bytes=58 * 1024 * 1024),
         cost_estimate=cost(3),
     )(group.reshape(1), samples)
+    columns, templates = lax.optimization_barrier((columns, templates))
     columns = lax.all_to_all(columns, TIME, 0, 0, tiled=True)
 
     block_index = jnp.arange(pattern.shape[1], dtype=jnp.int32)
@@ -537,8 +538,8 @@
     first = call(
         filter_first,
         shape(RANKS, 72, 128),
-        [smem] + [anywhere] * 9 + [vmem] * 6,
-        work + [mixing, pltpu.VMEM((GROUPS, RANKS, 8, 128), F32), pltpu.SemaphoreType.DMA((9,))],
+        [smem] + [anywhere] * 11 + [vmem] * 6,
+        work + [mixing, pltpu.VMEM((GROUPS, RANKS, 8, 128), F32), pltpu.SemaphoreType.DMA((11,))],
         cost_estimate=cost(8),
     )(jnp.stack((side, core)), *pieces, mix, bank, near, *tables, norm)
     first = lax.all_to_all(first, BINS, 0, 0, tiled=True)

time: 216 us -> 207 us (0.958)
  other arithmetic: 8.82 us -> 4.68 us
  starting transfers between devices: 60.1 us -> 57.3 us
    all_gather x1, waiting for transfers between devices: 13.9 us -> 5.96 us  [local(): others = lax.all_gather(others, ('zp', 'core'), axis=0)]
    ppermute x12 -> x13, waiting for transfers between devices: 10.7 us -> 15.3 us  [forward(): lax.ppermute(value, axis, [(i, (i + step) % 4) for i in range(4)])]
    all_to_all x1, starting transfers between devices: 8.38 us -> 5.89 us  [local(): second = lax.all_to_all(second, BINS, 0, 0, tiled=True)]
    mul x1, other arithmetic: 2.49 us -> 0.1 us  [local(): masked = jnp.swapaxes(templates.reshape(2, 4, 16, SIDE), 0, 1) * weight]
    all_to_all x1, waiting for transfers between devices: 0.01 us -> 2.3 us  [local(): first = lax.all_to_all(first, BINS, 0, 0, tiled=True)]
    ppermute x12 -> x13, starting transfers between devices: 31 us -> 32 us  [forward(): lax.ppermute(value, axis, [(i, (i + step) % 4) for i in range(4)])]
  transfers between devices with their start and end apart: 21 -> 23, of which waited for: 12 -> 14; matrix products, arithmetic and copies ran while one was open for 3% -> 2% of each run, Pallas kernels for 10% -> 10%
where the time goes in v2:
time: 207 us; the launch traced here: 206 us
  starting transfers between devices  57.3 us (28%)
  waiting for transfers between devices  49.4 us (24%)
  blocking collectives  47.5 us (23%)
  Pallas kernels  27.7 us (13%)
  between operations  15.4 us (7%)
  other arithmetic  4.68 us (2%)
  local copies, waits for them, and re-layouts  4.2 us (2%)
    ppermute x13, starting transfers between devices, forward(): lax.ppermute(value, axis, [(i, (i + step) % 4) for i in range(4)])  32 us
    all_to_all x1, blocking collectives, local(): power = lax.all_to_all(power, BINS, 0, 0, tiled=True)  24.1 us
    all_to_all x1, blocking collectives, first_bins(): return lax.all_to_all(rows.reshape(RANKS, 24, 128), BINS, 0, 0, tiled=True)  23.4 us
    all_to_all x1, waiting for transfers between devices, local(): second = lax.all_to_all(second, BINS, 0, 0, tiled=True)  22.9 us
    ppermute x13, waiting for transfers between devices, forward(): lax.ppermute(value, axis, [(i, (i + step) % 4) for i in range(4)])  15.3 us
    all_to_all x1, starting transfers between devices, local(): columns = lax.all_to_all(columns, TIME, 0, 0, tiled=True)  11.2 us
    pallas_call x1, Pallas kernels, local(): call(filter_rest, shape(RANKS, 128, 128), [anywhere] * 7, work + [pltpu.V...  9.87 us
    all_to_all x1, starting transfers between devices, local(): first = lax.all_to_all(first, BINS, 0, 0, tiled=True)  7.01 us
  transfers between devices with their start and end apart: 23, of which 14 were waited for; matrix products, arithmetic and copies ran while one was open for 2% of the time, Pallas kernels for 10%

profile of v2, /device:TPU:32, one launch (start us, length us, event | category | flops | bytes accessed | tf_op | source)
XLA Modules:
  0.0 206.1 jit_solution(10409215749929826031)
XLA Ops:
  10.8 3.1 %collective-permute-start.2 = (f32[2,16,2048]{2,1,0:T(8,128)S(1)}, f32[2,16,2048]{2,1,0:T(8,128)S(1)}, u32[]{:S(2)}, u32[]{:S(2)}) collective-permute-start(f32[2,16,2048]{2,1,0:T(8,128)S(1)} %get-tuple-element.92), channel_id=1, source_target_pairs={{0,6},{2,0},{4,2},{6,4},{1,7},{3,1},{5,3},{7,5},{8,14},{10,8},{12,... | collective-permute-start | bytes 786440 | tf_op jit(solution)/shard_map/ppermute | solution.py:451
  15.5 11.2 %all-to-all-start.1 = ((f32[32,24,128]{2,1,0:T(8,128)}), f32[32,24,128]{2,1,0:T(8,128)S(1)}, u32[]{:S(2)}, u32[]{:S(2)}) async-start(f32[32,24,128]{2,1,0:T(8,128)} %shard_map.131), calls=%async_computation.1 | async-start | bytes 786432 | tf_op jit(solution)/shard_map/all_to_all | solution.py:494
  29.0 3.3 %collective-permute-start.3 = (f32[2,16,2048]{2,1,0:T(8,128)S(1)}, f32[2,16,2048]{2,1,0:T(8,128)S(1)}, u32[]{:S(2)}, u32[]{:S(2)}) collective-permute-start(f32[2,16,2048]{2,1,0:T(8,128)S(1)} %get-tuple-element.89), channel_id=1, source_target_pairs={{0,64},{64,128},{128,192},{192,0},{1,65},{65,129},{129,193},{193,1... | collective-permute-start | bytes 786440 | tf_op jit(solution)/shard_map/ppermute | solution.py:451
  32.3 4.5 %collective-permute-start.4 = (f32[2,16,2048]{2,1,0:T(8,128)S(1)}, f32[2,16,2048]{2,1,0:T(8,128)S(1)}, u32[]{:S(2)}, u32[]{:S(2)}) collective-permute-start(f32[2,16,2048]{2,1,0:T(8,128)S(1)} %get-tuple-element.88), channel_id=1, source_target_pairs={{0,128},{64,192},{128,0},{192,64},{1,129},{65,193},{129,1},{193,65... | collective-permute-start | bytes 786440 | tf_op jit(solution)/shard_map/ppermute | solution.py:451
  36.8 2.7 %collective-permute-start.5 = (f32[2,16,2048]{2,1,0:T(8,128)S(1)}, f32[2,16,2048]{2,1,0:T(8,128)S(1)}, u32[]{:S(2)}, u32[]{:S(2)}) collective-permute-start(f32[2,16,2048]{2,1,0:T(8,128)S(1)} %get-tuple-element.87), channel_id=1, source_target_pairs={{0,192},{64,0},{128,64},{192,128},{1,193},{65,1},{129,65},{193,129... | collective-permute-start | bytes 786440 | tf_op jit(solution)/shard_map/ppermute | solution.py:451
  40.5 24.9 %conditional.1 = (f32[32,24,128]{2,1,0:T(8,128)S(1)}) conditional(s32[]{:T(128)} %convert_element_type.79, f32[32,24,128]{2,1,0:T(8,128)S(1)} %all-to-all-done.1, (f32[32,24,128]{2,1,0:T(8,128)S(1)}, f32[2,32,128]{2,1,0:T(8,128)S(1)}, bf16[2,256,256]{2,1,0:T(8,128)(2,1)S(1)}, bf16[2,128,128]{2,1,0:T(8,128)(2,1)S(1)}, ...), branch_computations={%region_0.1_spmd, %region_1.2_spmd} | conditional | flops 4000000000 | bytes 4786440 | solution.py:520
  42.0 23.4 %all_to_all.24 = f32[32,24,128]{2,1,0:T(8,128)S(1)} all-to-all(f32[32,24,128]{2,1,0:T(8,128)S(1)} %bitcast.55), channel_id=1, replica_groups=mesh['zp'=4,'zl'=2,'x'=4,'y'=4,'core'=2] {'zl','x','y'}, dimensions={0} | all-to-all | bytes 786432 | tf_op jit(solution)/shard_map/cond/branch_1_fun/all_to_all | solution.py:518
  66.1 2.4 %collective-permute-start.6 = (f32[32,8,128]{2,1,0:T(8,128)S(1)}, f32[32,8,128]{2,1,0:T(8,128)S(1)}, u32[]{:S(2)}, u32[]{:S(2)}) collective-permute-start(f32[32,8,128]{2,1,0:T(8,128)S(1)} %slice.13.refs_0_), channel_id=1, source_target_pairs={{0,64},{64,128},{128,192},{192,0},{1,65},{65,129},{129,193},{193,1... | collective-permute-start | bytes 393224 | tf_op jit(solution)/shard_map/ppermute | solution.py:451
  70.5 2.4 %fusion.8 = (f32[1,8,128,128]{3,2,1,0:T(8,128)S(1)}, f32[1,8,128,128]{3,2,1,0:T(8,128)S(1)}) fusion(s32[128,128]{1,0:T(8,128)S(1)} %get-tuple-element.108, s32[128,128]{1,0:T(8,128)S(1)} %get-tuple-element.107, s32[128]{0:T(128)S(1)} %add_add_fusion, s32[8,128]{1,0:T(8,128)S(1)} %get-tuple-element.106, s32[8,128]{1,0:T(8,128)S(1)} %get-tuple-element.105, ...), kind=kLoop, calls=%fused_computation.26 | loop fusion | flops 3932160 | bytes 1188864 | tf_op jit(solution)/shard_map/cos | solution.py:73
  77.1 3.2 %collective-permute-start.9 = (f32[16,8,128]{2,1,0:T(8,128)S(1)}, f32[16,8,128]{2,1,0:T(8,128)S(1)}, u32[]{:S(2)}, u32[]{:S(2)}) collective-permute-start(f32[16,8,128]{2,1,0:T(8,128)S(1)} %slice.17), channel_id=1, source_target_pairs={{0,192},{64,0},{128,64},{192,128},{1,193},{65,1},{129,65},{193,129... | collective-permute-start | bytes 196616 | tf_op jit(solution)/shard_map/ppermute | solution.py:451
  85.9 6.8 %shard_map.134 = f32[32,72,128]{2,1,0:T(8,128)} custom-call(s32[2]{0:T(128)S(1)} %pad_add_fusion.member_ref, f32[32,8,128]{2,1,0:T(8,128)S(1)} %slice.13.refs_0_, f32[32,8,128]{2,1,0:T(8,128)S(1)} %collective-permute-done.6.refs_1_, f32[32,8,128]{2,1,0:T(8,128)S(1)} %collective-permute-done.7.refs_2_, f32[16,8,128]{2,1,0:T(8,128)S(1)} %collective-permute-done.8.refs_3_, ...), custom_call_target="tpu_custom_call" | custom-call | flops 8000000000 | bytes 8000000 | tf_op jit(solution)/shard_map/pallas_call | solution.py:538
  92.7 7.0 %all-to-all-start.3 = ((f32[32,72,128]{2,1,0:T(8,128)}), f32[32,72,128]{2,1,0:T(8,128)S(1)}, u32[]{:S(2)}, u32[]{:S(2)}) async-start(f32[32,72,128]{2,1,0:T(8,128)} %shard_map.134), calls=%async_computation.3 | async-start | bytes 2359296 | tf_op jit(solution)/shard_map/all_to_all | solution.py:545
  99.7 6.0 %all-gather.3.cloned.1.call-done = f32[256,16,128]{2,1,0:T(8,128)} async-done(((f32[32,16,128]{2,1,0:T(8,128)}), f32[256,16,128]{2,1,0:T(8,128)}) %all-gather.3.cloned.1.call-update) | async-done | bytes 2097168 | tf_op jit(solution)/shard_map/all_gather | solution.py:534
  105.7 9.9 %shard_map.133 = f32[32,128,128]{2,1,0:T(8,128)} custom-call(f32[8,32,16,128]{3,2,1,0:T(8,128)} %bitcast.62, f32[2,2048,128]{2,1,0:T(8,128)} %copy-done.7, f32[2,128,128]{2,1,0:T(8,128)} %copy-done.1, bf16[2,8,256,256]{3,2,1,0:T(8,128)(2,1)} %copy-done, bf16[2,2,256,256]{3,2,1,0:T(8,128)(2,1)} %constant.332.clone.table_hbm.refs_13_, ...), custom_call_target="tpu_custom_call" | custom-call | flops 12000000000 | bytes 12000000 | tf_op jit(solution)/shard_map/pallas_call | solution.py:546
  115.6 2.3 %all-to-all-done.3.in_ref = f32[32,72,128]{2,1,0:T(8,128)S(1)} async-done(((f32[32,72,128]{2,1,0:T(8,128)}), f32[32,72,128]{2,1,0:T(8,128)S(1)}, u32[]{:S(2)}, u32[]{:S(2)}) %all-to-all-start.3) | async-done | bytes 1179680 | tf_op jit(solution)/shard_map/all_to_all | solution.py:545
  117.9 5.9 %all-to-all-start.2 = ((f32[32,128,128]{2,1,0:T(8,128)}), f32[32,128,128]{2,1,0:T(8,128)S(1)}, u32[]{:S(2)}, u32[]{:S(2)}) async-start(f32[32,128,128]{2,1,0:T(8,128)} %shard_map.133), calls=%async_computation.2 | async-start | bytes 4194304 | tf_op jit(solution)/shard_map/all_to_all | solution.py:564
  124.6 2.2 %shard_map.135.sum_ref = f32[1096,128]{1,0:T(8,128)S(1)} custom-call(f32[32,72,128]{2,1,0:T(8,128)S(1)} %all-to-all-done.3.in_ref, f32[2,32,128]{2,1,0:T(8,128)S(1)} %copy-done.5, bf16[2,256,256]{2,1,0:T(8,128)(2,1)S(1)} %copy-done.4), custom_call_target="tpu_custom_call" | custom-call | flops 3000000000 | bytes 3000000 | tf_op jit(solution)/shard_map/pallas_call | solution.py:568
  127.7 22.9 %all-to-all-done.2.in_ref = f32[32,128,128]{2,1,0:T(8,128)S(1)} async-done(((f32[32,128,128]{2,1,0:T(8,128)}), f32[32,128,128]{2,1,0:T(8,128)S(1)}, u32[]{:S(2)}, u32[]{:S(2)}) %all-to-all-start.2) | async-done | bytes 2097184 | tf_op jit(solution)/shard_map/all_to_all | solution.py:564
  151.6 2.2 %shard_map.136 = f32[1024,128]{1,0:T(8,128)S(1)} custom-call(f32[32,128,128]{2,1,0:T(8,128)S(1)} %all-to-all-done.2.in_ref, bf16[2,256,256]{2,1,0:T(8,128)(2,1)S(1)} %copy-done.4, f32[1096,128]{1,0:T(8,128)S(1)} %copy-done.9), custom_call_target="tpu_custom_call" | custom-call | flops 6000000000 | bytes 6000000 | tf_op jit(solution)/shard_map/pallas_call | solution.py:569
  153.9 3.3 %collective-permute-start.15 = (f32[256,128]{1,0:T(8,128)S(1)}, f32[256,128]{1,0:T(8,128)S(1)}, u32[]{:S(2)}, u32[]{:S(2)}) collective-permute-start(f32[256,128]{1,0:T(8,128)S(1)} %get-tuple-element.97), channel_id=1, source_target_pairs={{0,64},{64,128},{128,192},{192,0},{1,65},{65,129},{129,193},{193,1... | collective-permute-start | bytes 393224 | tf_op jit(solution)/shard_map/ppermute | solution.py:451
  157.3 5.1 %collective-permute-start.16 = (f32[256,128]{1,0:T(8,128)S(1)}, f32[256,128]{1,0:T(8,128)S(1)}, u32[]{:S(2)}, u32[]{:S(2)}) collective-permute-start(f32[256,128]{1,0:T(8,128)S(1)} %get-tuple-element.96), channel_id=1, source_target_pairs={{0,128},{64,192},{128,0},{192,64},{1,129},{65,193},{129,1},{193,65... | collective-permute-start | bytes 393224 | tf_op jit(solution)/shard_map/ppermute | solution.py:451
  162.3 4.6 %collective-permute-done.15.refs_1_ = f32[256,128]{1,0:T(8,128)S(1)} collective-permute-done((f32[256,128]{1,0:T(8,128)S(1)}, f32[256,128]{1,0:T(8,128)S(1)}, u32[]{:S(2)}, u32[]{:S(2)}) %collective-permute-start.15) | collective-permute-done | bytes 131104 | tf_op jit(solution)/shard_map/ppermute | solution.py:451
  169.0 2.8 %collective-permute-done.17.refs_3_ = f32[256,128]{1,0:T(8,128)S(1)} collective-permute-done((f32[256,128]{1,0:T(8,128)S(1)}, f32[256,128]{1,0:T(8,128)S(1)}, u32[]{:S(2)}, u32[]{:S(2)}) %collective-permute-start.17) | collective-permute-done | bytes 131104 | tf_op jit(solution)/shard_map/ppermute | solution.py:451
  173.4 24.1 %all_to_all.25.in_ref = f32[32,64,128]{2,1,0:T(8,128)S(1)} all-to-all(f32[32,64,128]{2,1,0:T(8,128)S(1)} %shard_map.138), channel_id=1, replica_groups=mesh['zp'=4,'zl'=2,'x'=4,'y'=4,'core'=2] {'zl','x','y'}, dimensions={0} | all-to-all | bytes 2097152 | tf_op jit(solution)/shard_map/all_to_all | solution.py:577
  (99 shorter events, 29.6 us)
Async XLA Ops:
  10.8 16.2 %collective-permute-start.2 = (f32[2,16,2048]{2,1,0:T(8,128)S(1)}, f32[2,16,2048]{2,1,0:T(8,128)S(1)}, u32[]{:S(2)}, u32[]{:S(2)}) collective-permute-start(f32[2,16,2048]{2,1,0:T(8,128)S(1)} %get-tuple-element.92), channel_id=1, source_target_pairs={{0,6},{2,0},{4,2},{6,4},{1,7},{3,1},{5,3},{7,5},{8,14},{10,8},{12,... | collective-permute-start | bytes 786440 | tf_op jit(solution)/shard_map/ppermute | solution.py:451
  13.8 13.1 %collective-permute-start.1 = (f32[2,16,2048]{2,1,0:T(8,128)S(1)}, f32[2,16,2048]{2,1,0:T(8,128)S(1)}, u32[]{:S(2)}, u32[]{:S(2)}) collective-permute-start(f32[2,16,2048]{2,1,0:T(8,128)S(1)} %get-tuple-element.93), channel_id=1, source_target_pairs={{0,4},{2,6},{4,0},{6,2},{1,5},{3,7},{5,1},{7,3},{8,12},{10,14},{12... | collective-permute-start | bytes 786440 | tf_op jit(solution)/shard_map/ppermute | solution.py:451
  14.5 14.3 %collective-permute-start = (f32[2,16,2048]{2,1,0:T(8,128)S(1)}, f32[2,16,2048]{2,1,0:T(8,128)S(1)}, u32[]{:S(2)}, u32[]{:S(2)}) collective-permute-start(f32[2,16,2048]{2,1,0:T(8,128)S(1)} %get-tuple-element.94), channel_id=1, source_target_pairs={{0,2},{2,4},{4,6},{6,0},{1,3},{3,5},{5,7},{7,1},{8,10},{10,12},{12... | collective-permute-start | bytes 786440 | tf_op jit(solution)/shard_map/ppermute | solution.py:451
  15.5 25.1 %all-to-all-start.1 = ((f32[32,24,128]{2,1,0:T(8,128)}), f32[32,24,128]{2,1,0:T(8,128)S(1)}, u32[]{:S(2)}, u32[]{:S(2)}) async-start(f32[32,24,128]{2,1,0:T(8,128)} %shard_map.131), calls=%async_computation.1 | async-start | bytes 786432 | tf_op jit(solution)/shard_map/all_to_all | solution.py:494
  26.6 79.0 %all-gather.3.cloned.1.call-start = ((), (), s32[]{:S(2)}) async-start(), calls=%async_computation.5 | async-start | bytes 2359296 | tf_op jit(solution)/shard_map/all_gather | solution.py:534
  29.0 36.4 %collective-permute-start.3 = (f32[2,16,2048]{2,1,0:T(8,128)S(1)}, f32[2,16,2048]{2,1,0:T(8,128)S(1)}, u32[]{:S(2)}, u32[]{:S(2)}) collective-permute-start(f32[2,16,2048]{2,1,0:T(8,128)S(1)} %get-tuple-element.89), channel_id=1, source_target_pairs={{0,64},{64,128},{128,192},{192,0},{1,65},{65,129},{129,193},{193,1... | collective-permute-start | bytes 786440 | tf_op jit(solution)/shard_map/ppermute | solution.py:451
  32.3 33.1 %collective-permute-start.4 = (f32[2,16,2048]{2,1,0:T(8,128)S(1)}, f32[2,16,2048]{2,1,0:T(8,128)S(1)}, u32[]{:S(2)}, u32[]{:S(2)}) collective-permute-start(f32[2,16,2048]{2,1,0:T(8,128)S(1)} %get-tuple-element.88), channel_id=1, source_target_pairs={{0,128},{64,192},{128,0},{192,64},{1,129},{65,193},{129,1},{193,65... | collective-permute-start | bytes 786440 | tf_op jit(solution)/shard_map/ppermute | solution.py:451
  36.8 28.6 %collective-permute-start.5 = (f32[2,16,2048]{2,1,0:T(8,128)S(1)}, f32[2,16,2048]{2,1,0:T(8,128)S(1)}, u32[]{:S(2)}, u32[]{:S(2)}) collective-permute-start(f32[2,16,2048]{2,1,0:T(8,128)S(1)} %get-tuple-element.87), channel_id=1, source_target_pairs={{0,192},{64,0},{128,64},{192,128},{1,193},{65,1},{129,65},{193,129... | collective-permute-start | bytes 786440 | tf_op jit(solution)/shard_map/ppermute | solution.py:451
  66.1 10.0 %collective-permute-start.6 = (f32[32,8,128]{2,1,0:T(8,128)S(1)}, f32[32,8,128]{2,1,0:T(8,128)S(1)}, u32[]{:S(2)}, u32[]{:S(2)}) collective-permute-start(f32[32,8,128]{2,1,0:T(8,128)S(1)} %slice.13.refs_0_), channel_id=1, source_target_pairs={{0,64},{64,128},{128,192},{192,0},{1,65},{65,129},{129,193},{193,1... | collective-permute-start | bytes 393224 | tf_op jit(solution)/shard_map/ppermute | solution.py:451
  68.5 8.6 %collective-permute-start.7 = (f32[32,8,128]{2,1,0:T(8,128)S(1)}, f32[32,8,128]{2,1,0:T(8,128)S(1)}, u32[]{:S(2)}, u32[]{:S(2)}) collective-permute-start(f32[32,8,128]{2,1,0:T(8,128)S(1)} %slice.13.refs_0_), channel_id=1, source_target_pairs={{0,192},{64,0},{128,64},{192,128},{1,193},{65,1},{129,65},{193,129... | collective-permute-start | bytes 393224 | tf_op jit(solution)/shard_map/ppermute | solution.py:451
  75.3 17.4 %copy-start = (bf16[2,8,256,256]{3,2,1,0:T(8,128)(2,1)}, bf16[2,8,256,256]{3,2,1,0:T(8,128)(2,1)S(1)}, u32[]{:S(2)}) copy-start(bf16[2,8,256,256]{3,2,1,0:T(8,128)(2,1)S(1)} %pad_maximum_fusion.1.mix_hbm.refs_10_) | copy-start | bytes 6291460
  76.1 6.4 %collective-permute-start.8 = (f32[16,8,128]{2,1,0:T(8,128)S(1)}, f32[16,8,128]{2,1,0:T(8,128)S(1)}, u32[]{:S(2)}, u32[]{:S(2)}) collective-permute-start(f32[16,8,128]{2,1,0:T(8,128)S(1)} %slice.16), channel_id=1, source_target_pairs={{0,64},{64,128},{128,192},{192,0},{1,65},{65,129},{129,193},{193,1... | collective-permute-start | bytes 196616 | tf_op jit(solution)/shard_map/ppermute | solution.py:451
  77.1 6.4 %collective-permute-start.9 = (f32[16,8,128]{2,1,0:T(8,128)S(1)}, f32[16,8,128]{2,1,0:T(8,128)S(1)}, u32[]{:S(2)}, u32[]{:S(2)}) collective-permute-start(f32[16,8,128]{2,1,0:T(8,128)S(1)} %slice.17), channel_id=1, source_target_pairs={{0,192},{64,0},{128,64},{192,128},{1,193},{65,1},{129,65},{193,129... | collective-permute-start | bytes 196616 | tf_op jit(solution)/shard_map/ppermute | solution.py:451
  83.6 2.3 %collective-permute-start.10 = (f32[32,8,128]{2,1,0:T(8,128)S(1)}, f32[32,8,128]{2,1,0:T(8,128)S(1)}, u32[]{:S(2)}, u32[]{:S(2)}) collective-permute-start(f32[32,8,128]{2,1,0:T(8,128)S(1)} %slice.13.refs_0_), channel_id=1, source_target_pairs={{0,1},{1,0},{2,3},{3,2},{4,5},{5,4},{6,7},{7,6},{8,9},{9,8},{10,11... | collective-permute-start | bytes 393224 | tf_op jit(solution)/shard_map/ppermute | solution.py:459
  83.6 2.3 %collective-permute-start.11 = (f32[32,8,128]{2,1,0:T(8,128)S(1)}, f32[32,8,128]{2,1,0:T(8,128)S(1)}, u32[]{:S(2)}, u32[]{:S(2)}) collective-permute-start(f32[32,8,128]{2,1,0:T(8,128)S(1)} %collective-permute-done.6.refs_1_), channel_id=1, source_target_pairs={{0,1},{1,0},{2,3},{3,2},{4,5},{5,4},{6,7},{7,6},{8,9},{9,8},{10,11... | collective-permute-start | bytes 393224 | tf_op jit(solution)/shard_map/ppermute | solution.py:459
  84.1 1.8 collective-permute-start.12
  84.1 1.4 collective-permute-start.13
  84.6 1.3 collective-permute-start.14
  92.7 25.2 %all-to-all-start.3 = ((f32[32,72,128]{2,1,0:T(8,128)}), f32[32,72,128]{2,1,0:T(8,128)S(1)}, u32[]{:S(2)}, u32[]{:S(2)}) async-start(f32[32,72,128]{2,1,0:T(8,128)} %shard_map.134), calls=%async_computation.3 | async-start | bytes 2359296 | tf_op jit(solution)/shard_map/all_to_all | solution.py:545
  117.9 32.7 %all-to-all-start.2 = ((f32[32,128,128]{2,1,0:T(8,128)}), f32[32,128,128]{2,1,0:T(8,128)S(1)}, u32[]{:S(2)}, u32[]{:S(2)}) async-start(f32[32,128,128]{2,1,0:T(8,128)} %shard_map.133), calls=%async_computation.2 | async-start | bytes 4194304 | tf_op jit(solution)/shard_map/all_to_all | solution.py:564
  153.9 13.0 %collective-permute-start.15 = (f32[256,128]{1,0:T(8,128)S(1)}, f32[256,128]{1,0:T(8,128)S(1)}, u32[]{:S(2)}, u32[]{:S(2)}) collective-permute-start(f32[256,128]{1,0:T(8,128)S(1)} %get-tuple-element.97), channel_id=1, source_target_pairs={{0,64},{64,128},{128,192},{192,0},{1,65},{65,129},{129,193},{193,1... | collective-permute-start | bytes 393224 | tf_op jit(solution)/shard_map/ppermute | solution.py:451
  157.3 11.8 %collective-permute-start.16 = (f32[256,128]{1,0:T(8,128)S(1)}, f32[256,128]{1,0:T(8,128)S(1)}, u32[]{:S(2)}, u32[]{:S(2)}) collective-permute-start(f32[256,128]{1,0:T(8,128)S(1)} %get-tuple-element.96), channel_id=1, source_target_pairs={{0,128},{64,192},{128,0},{192,64},{1,129},{65,193},{129,1},{193,65... | collective-permute-start | bytes 393224 | tf_op jit(solution)/shard_map/ppermute | solution.py:451
  162.3 9.5 %collective-permute-start.17 = (f32[256,128]{1,0:T(8,128)S(1)}, f32[256,128]{1,0:T(8,128)S(1)}, u32[]{:S(2)}, u32[]{:S(2)}) collective-permute-start(f32[256,128]{1,0:T(8,128)S(1)} %get-tuple-element.95), channel_id=1, source_target_pairs={{0,192},{64,0},{128,64},{192,128},{1,193},{65,1},{129,65},{193,129... | collective-permute-start | bytes 393224 | tf_op jit(solution)/shard_map/ppermute | solution.py:451
  171.8 1.4 collective-permute-start.18
  (14 other events, 108.1 us)
Sparse Core Ops, SparseCore 0:
  70.5 35.1 all-gather.2

commit v3 on v2

--- a/solution.py
+++ b/solution.py
@@ -258,7 +258,7 @@
             work_ref[pair // 2, tile_rows(128 + 8 * low), lanes] = im * cosine - re * sine
         return carry
 
-    lax.fori_loop(0, 16, spread, 0, unroll=2)
+    lax.fori_loop(0, 16, spread, 0, unroll=4)
     for copy in waits[0]:
         copy.wait()
 
@@ -292,7 +292,7 @@
             last_ref[k, tile_rows(8 * step), 128:256] = im
         return carry
 
-    lax.fori_loop(0, 16, collect, 0, unroll=2)
+    lax.fori_loop(0, 16, collect, 0, unroll=4)
     for copy in waits[1]:
         copy.wait()
     for k in range(8):
@@ -356,7 +356,7 @@
             work_ref[rows, 128:256] = im * cosine + re * sine
         return carry
 
-    lax.fori_loop(0, 4, step_fn, 0)
+    lax.fori_loop(0, 4, step_fn, 0, unroll=2)
 
     def power_of(quad):
         high, low = halves(work_ref[pl.ds(pl.multiple_of(128 * quad, 128), 128), :])

time: 207 us -> 206 us (level)
  no operation moved by 1% of the time
where the time goes in v3:
time: 206 us
  starting transfers between devices  57.2 us (28%)
  waiting for transfers between devices  49.1 us (24%)
  blocking collectives  48.5 us (24%)
  Pallas kernels  26.6 us (13%)
  between operations  15.4 us (7%)
  other arithmetic  4.68 us (2%)
  local copies, waits for them, and re-layouts  4.2 us (2%)
    ppermute x13, starting transfers between devices, forward(): lax.ppermute(value, axis, [(i, (i + step) % 4) for i in range(4)])  31.8 us
    all_to_all x1, blocking collectives, local(): power = lax.all_to_all(power, BINS, 0, 0, tiled=True)  25.1 us
    all_to_all x1, blocking collectives, first_bins(): return lax.all_to_all(rows.reshape(RANKS, 24, 128), BINS, 0, 0, tiled=True)  23.4 us
    all_to_all x1, waiting for transfers between devices, local(): second = lax.all_to_all(second, BINS, 0, 0, tiled=True)  22.9 us
    ppermute x13, waiting for transfers between devices, forward(): lax.ppermute(value, axis, [(i, (i + step) % 4) for i in range(4)])  14.3 us
    all_to_all x1, starting transfers between devices, local(): columns = lax.all_to_all(columns, TIME, 0, 0, tiled=True)  11.2 us
    pallas_call x1, Pallas kernels, local(): call(filter_rest, shape(RANKS, 128, 128), [anywhere] * 7, work + [pltpu.V...  9.23 us
    all_to_all x1, starting transfers between devices, local(): first = lax.all_to_all(first, BINS, 0, 0, tiled=True)  7.01 us
  transfers between devices with their start and end apart: 23, of which 14 were waited for; matrix products, arithmetic and copies ran while one was open for 2% of the time, Pallas kernels for 10%

profile of v3, /device:TPU:32, one launch (start us, length us, event | category | flops | bytes accessed | tf_op | source)
XLA Modules:
  0.0 205.6 jit_solution(14245735218754257696)
XLA Ops:
  7.2 2.1 %shard_map.131 = f32[32,24,128]{2,1,0:T(8,128)} custom-call(s32[1]{0:T(128)} %bitcast.2.group_ref, f32[192,32,128]{2,1,0:T(8,128)} %bitcast.61), custom_call_target="tpu_custom_call" | custom-call | flops 3000000000 | bytes 3000000 | tf_op jit(solution)/shard_map/pallas_call | solution.py:481
  10.8 3.1 %collective-permute-start.2 = (f32[2,16,2048]{2,1,0:T(8,128)S(1)}, f32[2,16,2048]{2,1,0:T(8,128)S(1)}, u32[]{:S(2)}, u32[]{:S(2)}) collective-permute-start(f32[2,16,2048]{2,1,0:T(8,128)S(1)} %get-tuple-element.92), channel_id=1, source_target_pairs={{0,6},{2,0},{4,2},{6,4},{1,7},{3,1},{5,3},{7,5},{8,14},{10,8},{12,... | collective-permute-start | bytes 786440 | tf_op jit(solution)/shard_map/ppermute | solution.py:451
  15.5 11.2 %all-to-all-start.1 = ((f32[32,24,128]{2,1,0:T(8,128)}), f32[32,24,128]{2,1,0:T(8,128)S(1)}, u32[]{:S(2)}, u32[]{:S(2)}) async-start(f32[32,24,128]{2,1,0:T(8,128)} %shard_map.131), calls=%async_computation.1 | async-start | bytes 786432 | tf_op jit(solution)/shard_map/all_to_all | solution.py:494
  29.0 3.3 %collective-permute-start.3 = (f32[2,16,2048]{2,1,0:T(8,128)S(1)}, f32[2,16,2048]{2,1,0:T(8,128)S(1)}, u32[]{:S(2)}, u32[]{:S(2)}) collective-permute-start(f32[2,16,2048]{2,1,0:T(8,128)S(1)} %get-tuple-element.89), channel_id=1, source_target_pairs={{0,64},{64,128},{128,192},{192,0},{1,65},{65,129},{129,193},{193,1... | collective-permute-start | bytes 786440 | tf_op jit(solution)/shard_map/ppermute | solution.py:451
  32.3 4.5 %collective-permute-start.4 = (f32[2,16,2048]{2,1,0:T(8,128)S(1)}, f32[2,16,2048]{2,1,0:T(8,128)S(1)}, u32[]{:S(2)}, u32[]{:S(2)}) collective-permute-start(f32[2,16,2048]{2,1,0:T(8,128)S(1)} %get-tuple-element.88), channel_id=1, source_target_pairs={{0,128},{64,192},{128,0},{192,64},{1,129},{65,193},{129,1},{193,65... | collective-permute-start | bytes 786440 | tf_op jit(solution)/shard_map/ppermute | solution.py:451
  36.8 2.7 %collective-permute-start.5 = (f32[2,16,2048]{2,1,0:T(8,128)S(1)}, f32[2,16,2048]{2,1,0:T(8,128)S(1)}, u32[]{:S(2)}, u32[]{:S(2)}) collective-permute-start(f32[2,16,2048]{2,1,0:T(8,128)S(1)} %get-tuple-element.87), channel_id=1, source_target_pairs={{0,192},{64,0},{128,64},{192,128},{1,193},{65,1},{129,65},{193,129... | collective-permute-start | bytes 786440 | tf_op jit(solution)/shard_map/ppermute | solution.py:451
  40.5 24.9 %conditional.1 = (f32[32,24,128]{2,1,0:T(8,128)S(1)}) conditional(s32[]{:T(128)} %convert_element_type.79, f32[32,24,128]{2,1,0:T(8,128)S(1)} %all-to-all-done.1, (f32[32,24,128]{2,1,0:T(8,128)S(1)}, f32[2,32,128]{2,1,0:T(8,128)S(1)}, bf16[2,256,256]{2,1,0:T(8,128)(2,1)S(1)}, bf16[2,128,128]{2,1,0:T(8,128)(2,1)S(1)}, ...), branch_computations={%region_0.1_spmd, %region_1.2_spmd} | conditional | flops 4000000000 | bytes 4786440 | solution.py:520
  42.0 23.4 %all_to_all.24 = f32[32,24,128]{2,1,0:T(8,128)S(1)} all-to-all(f32[32,24,128]{2,1,0:T(8,128)S(1)} %bitcast.55), channel_id=1, replica_groups=mesh['zp'=4,'zl'=2,'x'=4,'y'=4,'core'=2] {'zl','x','y'}, dimensions={0} | all-to-all | bytes 786432 | tf_op jit(solution)/shard_map/cond/branch_1_fun/all_to_all | solution.py:518
  66.1 2.4 %collective-permute-start.6 = (f32[32,8,128]{2,1,0:T(8,128)S(1)}, f32[32,8,128]{2,1,0:T(8,128)S(1)}, u32[]{:S(2)}, u32[]{:S(2)}) collective-permute-start(f32[32,8,128]{2,1,0:T(8,128)S(1)} %slice.13.refs_0_), channel_id=1, source_target_pairs={{0,64},{64,128},{128,192},{192,0},{1,65},{65,129},{129,193},{193,1... | collective-permute-start | bytes 393224 | tf_op jit(solution)/shard_map/ppermute | solution.py:451
  70.5 2.4 %fusion.8 = (f32[1,8,128,128]{3,2,1,0:T(8,128)S(1)}, f32[1,8,128,128]{3,2,1,0:T(8,128)S(1)}) fusion(s32[128,128]{1,0:T(8,128)S(1)} %get-tuple-element.108, s32[128,128]{1,0:T(8,128)S(1)} %get-tuple-element.107, s32[128]{0:T(128)S(1)} %add_add_fusion, s32[8,128]{1,0:T(8,128)S(1)} %get-tuple-element.106, s32[8,128]{1,0:T(8,128)S(1)} %get-tuple-element.105, ...), kind=kLoop, calls=%fused_computation.26 | loop fusion | flops 3932160 | bytes 1188864 | tf_op jit(solution)/shard_map/cos | solution.py:73
  77.1 3.2 %collective-permute-start.9 = (f32[16,8,128]{2,1,0:T(8,128)S(1)}, f32[16,8,128]{2,1,0:T(8,128)S(1)}, u32[]{:S(2)}, u32[]{:S(2)}) collective-permute-start(f32[16,8,128]{2,1,0:T(8,128)S(1)} %slice.17), channel_id=1, source_target_pairs={{0,192},{64,0},{128,64},{192,128},{1,193},{65,1},{129,65},{193,129... | collective-permute-start | bytes 196616 | tf_op jit(solution)/shard_map/ppermute | solution.py:451
  85.9 6.4 %shard_map.134 = f32[32,72,128]{2,1,0:T(8,128)} custom-call(s32[2]{0:T(128)S(1)} %pad_add_fusion.member_ref, f32[32,8,128]{2,1,0:T(8,128)S(1)} %slice.13.refs_0_, f32[32,8,128]{2,1,0:T(8,128)S(1)} %collective-permute-done.6.refs_1_, f32[32,8,128]{2,1,0:T(8,128)S(1)} %collective-permute-done.7.refs_2_, f32[16,8,128]{2,1,0:T(8,128)S(1)} %collective-permute-done.8.refs_3_, ...), custom_call_target="tpu_custom_call" | custom-call | flops 8000000000 | bytes 8000000 | tf_op jit(solution)/shard_map/pallas_call | solution.py:538
  92.3 7.0 %all-to-all-start.3 = ((f32[32,72,128]{2,1,0:T(8,128)}), f32[32,72,128]{2,1,0:T(8,128)S(1)}, u32[]{:S(2)}, u32[]{:S(2)}) async-start(f32[32,72,128]{2,1,0:T(8,128)} %shard_map.134), calls=%async_computation.3 | async-start | bytes 2359296 | tf_op jit(solution)/shard_map/all_to_all | solution.py:545
  99.3 6.6 %all-gather.3.cloned.1.call-done = f32[256,16,128]{2,1,0:T(8,128)} async-done(((f32[32,16,128]{2,1,0:T(8,128)}), f32[256,16,128]{2,1,0:T(8,128)}) %all-gather.3.cloned.1.call-update) | async-done | bytes 2097168 | tf_op jit(solution)/shard_map/all_gather | solution.py:534
  105.9 9.2 %shard_map.133 = f32[32,128,128]{2,1,0:T(8,128)} custom-call(f32[8,32,16,128]{3,2,1,0:T(8,128)} %bitcast.62, f32[2,2048,128]{2,1,0:T(8,128)} %copy-done.7, f32[2,128,128]{2,1,0:T(8,128)} %copy-done.1, bf16[2,8,256,256]{3,2,1,0:T(8,128)(2,1)} %copy-done, bf16[2,2,256,256]{3,2,1,0:T(8,128)(2,1)} %constant.332.clone.table_hbm.refs_13_, ...), custom_call_target="tpu_custom_call" | custom-call | flops 12000000000 | bytes 12000000 | tf_op jit(solution)/shard_map/pallas_call | solution.py:546
  115.1 2.4 %all-to-all-done.3.in_ref = f32[32,72,128]{2,1,0:T(8,128)S(1)} async-done(((f32[32,72,128]{2,1,0:T(8,128)}), f32[32,72,128]{2,1,0:T(8,128)S(1)}, u32[]{:S(2)}, u32[]{:S(2)}) %all-to-all-start.3) | async-done | bytes 1179680 | tf_op jit(solution)/shard_map/all_to_all | solution.py:545
  117.6 6.0 %all-to-all-start.2 = ((f32[32,128,128]{2,1,0:T(8,128)}), f32[32,128,128]{2,1,0:T(8,128)S(1)}, u32[]{:S(2)}, u32[]{:S(2)}) async-start(f32[32,128,128]{2,1,0:T(8,128)} %shard_map.133), calls=%async_computation.2 | async-start | bytes 4194304 | tf_op jit(solution)/shard_map/all_to_all | solution.py:564
  124.4 2.2 %shard_map.135.sum_ref = f32[1096,128]{1,0:T(8,128)S(1)} custom-call(f32[32,72,128]{2,1,0:T(8,128)S(1)} %all-to-all-done.3.in_ref, f32[2,32,128]{2,1,0:T(8,128)S(1)} %copy-done.5, bf16[2,256,256]{2,1,0:T(8,128)(2,1)S(1)} %copy-done.4), custom_call_target="tpu_custom_call" | custom-call | flops 3000000000 | bytes 3000000 | tf_op jit(solution)/shard_map/pallas_call | solution.py:568
  127.5 22.9 %all-to-all-done.2.in_ref = f32[32,128,128]{2,1,0:T(8,128)S(1)} async-done(((f32[32,128,128]{2,1,0:T(8,128)}), f32[32,128,128]{2,1,0:T(8,128)S(1)}, u32[]{:S(2)}, u32[]{:S(2)}) %all-to-all-start.2) | async-done | bytes 2097184 | tf_op jit(solution)/shard_map/all_to_all | solution.py:564
  151.5 2.2 %shard_map.136 = f32[1024,128]{1,0:T(8,128)S(1)} custom-call(f32[32,128,128]{2,1,0:T(8,128)S(1)} %all-to-all-done.2.in_ref, bf16[2,256,256]{2,1,0:T(8,128)(2,1)S(1)} %copy-done.4, f32[1096,128]{1,0:T(8,128)S(1)} %copy-done.9), custom_call_target="tpu_custom_call" | custom-call | flops 6000000000 | bytes 6000000 | tf_op jit(solution)/shard_map/pallas_call | solution.py:569
  153.7 2.1 %collective-permute-start.15 = (f32[256,128]{1,0:T(8,128)S(1)}, f32[256,128]{1,0:T(8,128)S(1)}, u32[]{:S(2)}, u32[]{:S(2)}) collective-permute-start(f32[256,128]{1,0:T(8,128)S(1)} %get-tuple-element.97), channel_id=1, source_target_pairs={{0,64},{64,128},{128,192},{192,0},{1,65},{65,129},{129,193},{193,1... | collective-permute-start | bytes 393224 | tf_op jit(solution)/shard_map/ppermute | solution.py:451
  155.9 6.0 %collective-permute-start.16 = (f32[256,128]{1,0:T(8,128)S(1)}, f32[256,128]{1,0:T(8,128)S(1)}, u32[]{:S(2)}, u32[]{:S(2)}) collective-permute-start(f32[256,128]{1,0:T(8,128)S(1)} %get-tuple-element.96), channel_id=1, source_target_pairs={{0,128},{64,192},{128,0},{192,64},{1,129},{65,193},{129,1},{193,65... | collective-permute-start | bytes 393224 | tf_op jit(solution)/shard_map/ppermute | solution.py:451
  161.9 4.8 %collective-permute-done.15.refs_1_ = f32[256,128]{1,0:T(8,128)S(1)} collective-permute-done((f32[256,128]{1,0:T(8,128)S(1)}, f32[256,128]{1,0:T(8,128)S(1)}, u32[]{:S(2)}, u32[]{:S(2)}) %collective-permute-start.15) | collective-permute-done | bytes 131104 | tf_op jit(solution)/shard_map/ppermute | solution.py:451
  171.9 25.1 %all_to_all.25.in_ref = f32[32,64,128]{2,1,0:T(8,128)S(1)} all-to-all(f32[32,64,128]{2,1,0:T(8,128)S(1)} %shard_map.138), channel_id=1, replica_groups=mesh['zp'=4,'zl'=2,'x'=4,'y'=4,'core'=2] {'zl','x','y'}, dimensions={0} | all-to-all | bytes 2097152 | tf_op jit(solution)/shard_map/all_to_all | solution.py:577
  (99 shorter events, 28.9 us)
Async XLA Ops:
  10.8 16.2 %collective-permute-start.2 = (f32[2,16,2048]{2,1,0:T(8,128)S(1)}, f32[2,16,2048]{2,1,0:T(8,128)S(1)}, u32[]{:S(2)}, u32[]{:S(2)}) collective-permute-start(f32[2,16,2048]{2,1,0:T(8,128)S(1)} %get-tuple-element.92), channel_id=1, source_target_pairs={{0,6},{2,0},{4,2},{6,4},{1,7},{3,1},{5,3},{7,5},{8,14},{10,8},{12,... | collective-permute-start | bytes 786440 | tf_op jit(solution)/shard_map/ppermute | solution.py:451
  13.8 13.1 %collective-permute-start.1 = (f32[2,16,2048]{2,1,0:T(8,128)S(1)}, f32[2,16,2048]{2,1,0:T(8,128)S(1)}, u32[]{:S(2)}, u32[]{:S(2)}) collective-permute-start(f32[2,16,2048]{2,1,0:T(8,128)S(1)} %get-tuple-element.93), channel_id=1, source_target_pairs={{0,4},{2,6},{4,0},{6,2},{1,5},{3,7},{5,1},{7,3},{8,12},{10,14},{12... | collective-permute-start | bytes 786440 | tf_op jit(solution)/shard_map/ppermute | solution.py:451
  14.5 14.3 %collective-permute-start = (f32[2,16,2048]{2,1,0:T(8,128)S(1)}, f32[2,16,2048]{2,1,0:T(8,128)S(1)}, u32[]{:S(2)}, u32[]{:S(2)}) collective-permute-start(f32[2,16,2048]{2,1,0:T(8,128)S(1)} %get-tuple-element.94), channel_id=1, source_target_pairs={{0,2},{2,4},{4,6},{6,0},{1,3},{3,5},{5,7},{7,1},{8,10},{10,12},{12... | collective-permute-start | bytes 786440 | tf_op jit(solution)/shard_map/ppermute | solution.py:451
  15.5 25.1 %all-to-all-start.1 = ((f32[32,24,128]{2,1,0:T(8,128)}), f32[32,24,128]{2,1,0:T(8,128)S(1)}, u32[]{:S(2)}, u32[]{:S(2)}) async-start(f32[32,24,128]{2,1,0:T(8,128)} %shard_map.131), calls=%async_computation.1 | async-start | bytes 786432 | tf_op jit(solution)/shard_map/all_to_all | solution.py:494
  26.6 79.2 %all-gather.3.cloned.1.call-start = ((), (), s32[]{:S(2)}) async-start(), calls=%async_computation.5 | async-start | bytes 2359296 | tf_op jit(solution)/shard_map/all_gather | solution.py:534
  29.0 36.4 %collective-permute-start.3 = (f32[2,16,2048]{2,1,0:T(8,128)S(1)}, f32[2,16,2048]{2,1,0:T(8,128)S(1)}, u32[]{:S(2)}, u32[]{:S(2)}) collective-permute-start(f32[2,16,2048]{2,1,0:T(8,128)S(1)} %get-tuple-element.89), channel_id=1, source_target_pairs={{0,64},{64,128},{128,192},{192,0},{1,65},{65,129},{129,193},{193,1... | collective-permute-start | bytes 786440 | tf_op jit(solution)/shard_map/ppermute | solution.py:451
  32.3 33.1 %collective-permute-start.4 = (f32[2,16,2048]{2,1,0:T(8,128)S(1)}, f32[2,16,2048]{2,1,0:T(8,128)S(1)}, u32[]{:S(2)}, u32[]{:S(2)}) collective-permute-start(f32[2,16,2048]{2,1,0:T(8,128)S(1)} %get-tuple-element.88), channel_id=1, source_target_pairs={{0,128},{64,192},{128,0},{192,64},{1,129},{65,193},{129,1},{193,65... | collective-permute-start | bytes 786440 | tf_op jit(solution)/shard_map/ppermute | solution.py:451
  36.8 28.6 %collective-permute-start.5 = (f32[2,16,2048]{2,1,0:T(8,128)S(1)}, f32[2,16,2048]{2,1,0:T(8,128)S(1)}, u32[]{:S(2)}, u32[]{:S(2)}) collective-permute-start(f32[2,16,2048]{2,1,0:T(8,128)S(1)} %get-tuple-element.87), channel_id=1, source_target_pairs={{0,192},{64,0},{128,64},{192,128},{1,193},{65,1},{129,65},{193,129... | collective-permute-start | bytes 786440 | tf_op jit(solution)/shard_map/ppermute | solution.py:451
  66.1 10.0 %collective-permute-start.6 = (f32[32,8,128]{2,1,0:T(8,128)S(1)}, f32[32,8,128]{2,1,0:T(8,128)S(1)}, u32[]{:S(2)}, u32[]{:S(2)}) collective-permute-start(f32[32,8,128]{2,1,0:T(8,128)S(1)} %slice.13.refs_0_), channel_id=1, source_target_pairs={{0,64},{64,128},{128,192},{192,0},{1,65},{65,129},{129,193},{193,1... | collective-permute-start | bytes 393224 | tf_op jit(solution)/shard_map/ppermute | solution.py:451
  68.5 8.6 %collective-permute-start.7 = (f32[32,8,128]{2,1,0:T(8,128)S(1)}, f32[32,8,128]{2,1,0:T(8,128)S(1)}, u32[]{:S(2)}, u32[]{:S(2)}) collective-permute-start(f32[32,8,128]{2,1,0:T(8,128)S(1)} %slice.13.refs_0_), channel_id=1, source_target_pairs={{0,192},{64,0},{128,64},{192,128},{1,193},{65,1},{129,65},{193,129... | collective-permute-start | bytes 393224 | tf_op jit(solution)/shard_map/ppermute | solution.py:451
  75.3 17.0 %copy-start = (bf16[2,8,256,256]{3,2,1,0:T(8,128)(2,1)}, bf16[2,8,256,256]{3,2,1,0:T(8,128)(2,1)S(1)}, u32[]{:S(2)}) copy-start(bf16[2,8,256,256]{3,2,1,0:T(8,128)(2,1)S(1)} %pad_maximum_fusion.1.mix_hbm.refs_10_) | copy-start | bytes 6291460
  76.1 6.4 %collective-permute-start.8 = (f32[16,8,128]{2,1,0:T(8,128)S(1)}, f32[16,8,128]{2,1,0:T(8,128)S(1)}, u32[]{:S(2)}, u32[]{:S(2)}) collective-permute-start(f32[16,8,128]{2,1,0:T(8,128)S(1)} %slice.16), channel_id=1, source_target_pairs={{0,64},{64,128},{128,192},{192,0},{1,65},{65,129},{129,193},{193,1... | collective-permute-start | bytes 196616 | tf_op jit(solution)/shard_map/ppermute | solution.py:451
  77.1 6.4 %collective-permute-start.9 = (f32[16,8,128]{2,1,0:T(8,128)S(1)}, f32[16,8,128]{2,1,0:T(8,128)S(1)}, u32[]{:S(2)}, u32[]{:S(2)}) collective-permute-start(f32[16,8,128]{2,1,0:T(8,128)S(1)} %slice.17), channel_id=1, source_target_pairs={{0,192},{64,0},{128,64},{192,128},{1,193},{65,1},{129,65},{193,129... | collective-permute-start | bytes 196616 | tf_op jit(solution)/shard_map/ppermute | solution.py:451
  83.6 2.3 %collective-permute-start.10 = (f32[32,8,128]{2,1,0:T(8,128)S(1)}, f32[32,8,128]{2,1,0:T(8,128)S(1)}, u32[]{:S(2)}, u32[]{:S(2)}) collective-permute-start(f32[32,8,128]{2,1,0:T(8,128)S(1)} %slice.13.refs_0_), channel_id=1, source_target_pairs={{0,1},{1,0},{2,3},{3,2},{4,5},{5,4},{6,7},{7,6},{8,9},{9,8},{10,11... | collective-permute-start | bytes 393224 | tf_op jit(solution)/shard_map/ppermute | solution.py:459
  83.6 2.3 %collective-permute-start.11 = (f32[32,8,128]{2,1,0:T(8,128)S(1)}, f32[32,8,128]{2,1,0:T(8,128)S(1)}, u32[]{:S(2)}, u32[]{:S(2)}) collective-permute-start(f32[32,8,128]{2,1,0:T(8,128)S(1)} %collective-permute-done.6.refs_1_), channel_id=1, source_target_pairs={{0,1},{1,0},{2,3},{3,2},{4,5},{5,4},{6,7},{7,6},{8,9},{9,8},{10,11... | collective-permute-start | bytes 393224 | tf_op jit(solution)/shard_map/ppermute | solution.py:459
  84.1 1.8 collective-permute-start.12
  84.1 1.4 collective-permute-start.13
  84.6 1.3 collective-permute-start.14
  92.3 25.3 %all-to-all-start.3 = ((f32[32,72,128]{2,1,0:T(8,128)}), f32[32,72,128]{2,1,0:T(8,128)S(1)}, u32[]{:S(2)}, u32[]{:S(2)}) async-start(f32[32,72,128]{2,1,0:T(8,128)} %shard_map.134), calls=%async_computation.3 | async-start | bytes 2359296 | tf_op jit(solution)/shard_map/all_to_all | solution.py:545
  117.6 32.8 %all-to-all-start.2 = ((f32[32,128,128]{2,1,0:T(8,128)}), f32[32,128,128]{2,1,0:T(8,128)S(1)}, u32[]{:S(2)}, u32[]{:S(2)}) async-start(f32[32,128,128]{2,1,0:T(8,128)} %shard_map.133), calls=%async_computation.2 | async-start | bytes 4194304 | tf_op jit(solution)/shard_map/all_to_all | solution.py:564
  153.7 13.0 %collective-permute-start.15 = (f32[256,128]{1,0:T(8,128)S(1)}, f32[256,128]{1,0:T(8,128)S(1)}, u32[]{:S(2)}, u32[]{:S(2)}) collective-permute-start(f32[256,128]{1,0:T(8,128)S(1)} %get-tuple-element.97), channel_id=1, source_target_pairs={{0,64},{64,128},{128,192},{192,0},{1,65},{65,129},{129,193},{193,1... | collective-permute-start | bytes 393224 | tf_op jit(solution)/shard_map/ppermute | solution.py:451
  155.9 12.4 %collective-permute-start.16 = (f32[256,128]{1,0:T(8,128)S(1)}, f32[256,128]{1,0:T(8,128)S(1)}, u32[]{:S(2)}, u32[]{:S(2)}) collective-permute-start(f32[256,128]{1,0:T(8,128)S(1)} %get-tuple-element.96), channel_id=1, source_target_pairs={{0,128},{64,192},{128,0},{192,64},{1,129},{65,193},{129,1},{193,65... | collective-permute-start | bytes 393224 | tf_op jit(solution)/shard_map/ppermute | solution.py:451
  161.9 8.4 %collective-permute-start.17 = (f32[256,128]{1,0:T(8,128)S(1)}, f32[256,128]{1,0:T(8,128)S(1)}, u32[]{:S(2)}, u32[]{:S(2)}) collective-permute-start(f32[256,128]{1,0:T(8,128)S(1)} %get-tuple-element.95), channel_id=1, source_target_pairs={{0,192},{64,0},{128,64},{192,128},{1,193},{65,1},{129,65},{193,129... | collective-permute-start | bytes 393224 | tf_op jit(solution)/shard_map/ppermute | solution.py:451
  170.3 1.4 collective-permute-start.18
  (14 other events, 108.0 us)
Sparse Core Ops, SparseCore 0:
  70.5 35.3 all-gather.2

commit v4 on v3

--- a/solution.py
+++ b/solution.py
@@ -258,7 +258,7 @@
             work_ref[pair // 2, tile_rows(128 + 8 * low), lanes] = im * cosine - re * sine
         return carry
 
-    lax.fori_loop(0, 16, spread, 0, unroll=4)
+    lax.fori_loop(0, 16, spread, 0, unroll=8)
     for copy in waits[0]:
         copy.wait()
 
@@ -292,7 +292,7 @@
             last_ref[k, tile_rows(8 * step), 128:256] = im
         return carry
 
-    lax.fori_loop(0, 16, collect, 0, unroll=4)
+    lax.fori_loop(0, 16, collect, 0, unroll=8)
     for copy in waits[1]:
         copy.wait()
     for k in range(8):

time: 206 us -> 206 us (level)
  no operation moved by 1% of the time
where the time goes in v4:
time: 206 us
  starting transfers between devices  56.9 us (28%)
  waiting for transfers between devices  49.5 us (24%)
  blocking collectives  48.6 us (24%)
  Pallas kernels  26.3 us (13%)
  between operations  15.4 us (7%)
  other arithmetic  4.68 us (2%)
  local copies, waits for them, and re-layouts  4.2 us (2%)
    ppermute x13, starting transfers between devices, forward(): lax.ppermute(value, axis, [(i, (i + step) % 4) for i in range(4)])  31.5 us
    all_to_all x1, blocking collectives, local(): power = lax.all_to_all(power, BINS, 0, 0, tiled=True)  25.2 us
    all_to_all x1, blocking collectives, first_bins(): return lax.all_to_all(rows.reshape(RANKS, 24, 128), BINS, 0, 0, tiled=True)  23.4 us
    all_to_all x1, waiting for transfers between devices, local(): second = lax.all_to_all(second, BINS, 0, 0, tiled=True)  23.1 us
    ppermute x13, waiting for transfers between devices, forward(): lax.ppermute(value, axis, [(i, (i + step) % 4) for i in range(4)])  14.2 us
    all_to_all x1, starting transfers between devices, local(): columns = lax.all_to_all(columns, TIME, 0, 0, tiled=True)  11.2 us
    pallas_call x1, Pallas kernels, local(): call(filter_rest, shape(RANKS, 128, 128), [anywhere] * 7, work + [pltpu.V...  9.09 us
    all_to_all x1, starting transfers between devices, local(): first = lax.all_to_all(first, BINS, 0, 0, tiled=True)  7.01 us
  transfers between devices with their start and end apart: 23, of which 14 were waited for; matrix products, arithmetic and copies ran while one was open for 2% of the time, Pallas kernels for 10%

profile of v4, /device:TPU:32, one launch (start us, length us, event | category | flops | bytes accessed | tf_op | source)
XLA Modules:
  0.0 205.5 jit_solution(4933453734329972721)
XLA Ops:
  10.8 3.1 %collective-permute-start.2 = (f32[2,16,2048]{2,1,0:T(8,128)S(1)}, f32[2,16,2048]{2,1,0:T(8,128)S(1)}, u32[]{:S(2)}, u32[]{:S(2)}) collective-permute-start(f32[2,16,2048]{2,1,0:T(8,128)S(1)} %get-tuple-element.92), channel_id=1, source_target_pairs={{0,6},{2,0},{4,2},{6,4},{1,7},{3,1},{5,3},{7,5},{8,14},{10,8},{12,... | collective-permute-start | bytes 786440 | tf_op jit(solution)/shard_map/ppermute | solution.py:451
  15.5 11.2 %all-to-all-start.1 = ((f32[32,24,128]{2,1,0:T(8,128)}), f32[32,24,128]{2,1,0:T(8,128)S(1)}, u32[]{:S(2)}, u32[]{:S(2)}) async-start(f32[32,24,128]{2,1,0:T(8,128)} %shard_map.131), calls=%async_computation.1 | async-start | bytes 786432 | tf_op jit(solution)/shard_map/all_to_all | solution.py:494
  29.0 3.3 %collective-permute-start.3 = (f32[2,16,2048]{2,1,0:T(8,128)S(1)}, f32[2,16,2048]{2,1,0:T(8,128)S(1)}, u32[]{:S(2)}, u32[]{:S(2)}) collective-permute-start(f32[2,16,2048]{2,1,0:T(8,128)S(1)} %get-tuple-element.89), channel_id=1, source_target_pairs={{0,64},{64,128},{128,192},{192,0},{1,65},{65,129},{129,193},{193,1... | collective-permute-start | bytes 786440 | tf_op jit(solution)/shard_map/ppermute | solution.py:451
  32.3 4.5 %collective-permute-start.4 = (f32[2,16,2048]{2,1,0:T(8,128)S(1)}, f32[2,16,2048]{2,1,0:T(8,128)S(1)}, u32[]{:S(2)}, u32[]{:S(2)}) collective-permute-start(f32[2,16,2048]{2,1,0:T(8,128)S(1)} %get-tuple-element.88), channel_id=1, source_target_pairs={{0,128},{64,192},{128,0},{192,64},{1,129},{65,193},{129,1},{193,65... | collective-permute-start | bytes 786440 | tf_op jit(solution)/shard_map/ppermute | solution.py:451
  36.8 2.7 %collective-permute-start.5 = (f32[2,16,2048]{2,1,0:T(8,128)S(1)}, f32[2,16,2048]{2,1,0:T(8,128)S(1)}, u32[]{:S(2)}, u32[]{:S(2)}) collective-permute-start(f32[2,16,2048]{2,1,0:T(8,128)S(1)} %get-tuple-element.87), channel_id=1, source_target_pairs={{0,192},{64,0},{128,64},{192,128},{1,193},{65,1},{129,65},{193,129... | collective-permute-start | bytes 786440 | tf_op jit(solution)/shard_map/ppermute | solution.py:451
  40.5 24.9 %conditional.1 = (f32[32,24,128]{2,1,0:T(8,128)S(1)}) conditional(s32[]{:T(128)} %convert_element_type.79, f32[32,24,128]{2,1,0:T(8,128)S(1)} %all-to-all-done.1, (f32[32,24,128]{2,1,0:T(8,128)S(1)}, f32[2,32,128]{2,1,0:T(8,128)S(1)}, bf16[2,256,256]{2,1,0:T(8,128)(2,1)S(1)}, bf16[2,128,128]{2,1,0:T(8,128)(2,1)S(1)}, ...), branch_computations={%region_0.1_spmd, %region_1.2_spmd} | conditional | flops 4000000000 | bytes 4786440 | solution.py:520
  42.0 23.4 %all_to_all.24 = f32[32,24,128]{2,1,0:T(8,128)S(1)} all-to-all(f32[32,24,128]{2,1,0:T(8,128)S(1)} %bitcast.55), channel_id=1, replica_groups=mesh['zp'=4,'zl'=2,'x'=4,'y'=4,'core'=2] {'zl','x','y'}, dimensions={0} | all-to-all | bytes 786432 | tf_op jit(solution)/shard_map/cond/branch_1_fun/all_to_all | solution.py:518
  66.1 2.4 %collective-permute-start.6 = (f32[32,8,128]{2,1,0:T(8,128)S(1)}, f32[32,8,128]{2,1,0:T(8,128)S(1)}, u32[]{:S(2)}, u32[]{:S(2)}) collective-permute-start(f32[32,8,128]{2,1,0:T(8,128)S(1)} %slice.13.refs_0_), channel_id=1, source_target_pairs={{0,64},{64,128},{128,192},{192,0},{1,65},{65,129},{129,193},{193,1... | collective-permute-start | bytes 393224 | tf_op jit(solution)/shard_map/ppermute | solution.py:451
  70.5 2.4 %fusion.8 = (f32[1,8,128,128]{3,2,1,0:T(8,128)S(1)}, f32[1,8,128,128]{3,2,1,0:T(8,128)S(1)}) fusion(s32[128,128]{1,0:T(8,128)S(1)} %get-tuple-element.108, s32[128,128]{1,0:T(8,128)S(1)} %get-tuple-element.107, s32[128]{0:T(128)S(1)} %add_add_fusion, s32[8,128]{1,0:T(8,128)S(1)} %get-tuple-element.106, s32[8,128]{1,0:T(8,128)S(1)} %get-tuple-element.105, ...), kind=kLoop, calls=%fused_computation.26 | loop fusion | flops 3932160 | bytes 1188864 | tf_op jit(solution)/shard_map/cos | solution.py:73
  77.1 3.2 %collective-permute-start.9 = (f32[16,8,128]{2,1,0:T(8,128)S(1)}, f32[16,8,128]{2,1,0:T(8,128)S(1)}, u32[]{:S(2)}, u32[]{:S(2)}) collective-permute-start(f32[16,8,128]{2,1,0:T(8,128)S(1)} %slice.17), channel_id=1, source_target_pairs={{0,192},{64,0},{128,64},{192,128},{1,193},{65,1},{129,65},{193,129... | collective-permute-start | bytes 196616 | tf_op jit(solution)/shard_map/ppermute | solution.py:451
  85.9 6.2 %shard_map.134 = f32[32,72,128]{2,1,0:T(8,128)} custom-call(s32[2]{0:T(128)S(1)} %pad_add_fusion.member_ref, f32[32,8,128]{2,1,0:T(8,128)S(1)} %slice.13.refs_0_, f32[32,8,128]{2,1,0:T(8,128)S(1)} %collective-permute-done.6.refs_1_, f32[32,8,128]{2,1,0:T(8,128)S(1)} %collective-permute-done.7.refs_2_, f32[16,8,128]{2,1,0:T(8,128)S(1)} %collective-permute-done.8.refs_3_, ...), custom_call_target="tpu_custom_call" | custom-call | flops 8000000000 | bytes 8000000 | tf_op jit(solution)/shard_map/pallas_call | solution.py:538
  92.2 7.0 %all-to-all-start.3 = ((f32[32,72,128]{2,1,0:T(8,128)}), f32[32,72,128]{2,1,0:T(8,128)S(1)}, u32[]{:S(2)}, u32[]{:S(2)}) async-start(f32[32,72,128]{2,1,0:T(8,128)} %shard_map.134), calls=%async_computation.3 | async-start | bytes 2359296 | tf_op jit(solution)/shard_map/all_to_all | solution.py:545
  99.2 6.9 %all-gather.3.cloned.1.call-done = f32[256,16,128]{2,1,0:T(8,128)} async-done(((f32[32,16,128]{2,1,0:T(8,128)}), f32[256,16,128]{2,1,0:T(8,128)}) %all-gather.3.cloned.1.call-update) | async-done | bytes 2097168 | tf_op jit(solution)/shard_map/all_gather | solution.py:534
  106.0 9.1 %shard_map.133 = f32[32,128,128]{2,1,0:T(8,128)} custom-call(f32[8,32,16,128]{3,2,1,0:T(8,128)} %bitcast.62, f32[2,2048,128]{2,1,0:T(8,128)} %copy-done.7, f32[2,128,128]{2,1,0:T(8,128)} %copy-done.1, bf16[2,8,256,256]{3,2,1,0:T(8,128)(2,1)} %copy-done, bf16[2,2,256,256]{3,2,1,0:T(8,128)(2,1)} %constant.332.clone.table_hbm.refs_13_, ...), custom_call_target="tpu_custom_call" | custom-call | flops 12000000000 | bytes 12000000 | tf_op jit(solution)/shard_map/pallas_call | solution.py:546
  115.2 2.4 %all-to-all-done.3.in_ref = f32[32,72,128]{2,1,0:T(8,128)S(1)} async-done(((f32[32,72,128]{2,1,0:T(8,128)}), f32[32,72,128]{2,1,0:T(8,128)S(1)}, u32[]{:S(2)}, u32[]{:S(2)}) %all-to-all-start.3) | async-done | bytes 1179680 | tf_op jit(solution)/shard_map/all_to_all | solution.py:545
  117.6 6.0 %all-to-all-start.2 = ((f32[32,128,128]{2,1,0:T(8,128)}), f32[32,128,128]{2,1,0:T(8,128)S(1)}, u32[]{:S(2)}, u32[]{:S(2)}) async-start(f32[32,128,128]{2,1,0:T(8,128)} %shard_map.133), calls=%async_computation.2 | async-start | bytes 4194304 | tf_op jit(solution)/shard_map/all_to_all | solution.py:564
  124.4 2.2 %shard_map.135.sum_ref = f32[1096,128]{1,0:T(8,128)S(1)} custom-call(f32[32,72,128]{2,1,0:T(8,128)S(1)} %all-to-all-done.3.in_ref, f32[2,32,128]{2,1,0:T(8,128)S(1)} %copy-done.5, bf16[2,256,256]{2,1,0:T(8,128)(2,1)S(1)} %copy-done.4), custom_call_target="tpu_custom_call" | custom-call | flops 3000000000 | bytes 3000000 | tf_op jit(solution)/shard_map/pallas_call | solution.py:568
  127.5 23.1 %all-to-all-done.2.in_ref = f32[32,128,128]{2,1,0:T(8,128)S(1)} async-done(((f32[32,128,128]{2,1,0:T(8,128)}), f32[32,128,128]{2,1,0:T(8,128)S(1)}, u32[]{:S(2)}, u32[]{:S(2)}) %all-to-all-start.2) | async-done | bytes 2097184 | tf_op jit(solution)/shard_map/all_to_all | solution.py:564
  151.6 2.2 %shard_map.136 = f32[1024,128]{1,0:T(8,128)S(1)} custom-call(f32[32,128,128]{2,1,0:T(8,128)S(1)} %all-to-all-done.2.in_ref, bf16[2,256,256]{2,1,0:T(8,128)(2,1)S(1)} %copy-done.4, f32[1096,128]{1,0:T(8,128)S(1)} %copy-done.9), custom_call_target="tpu_custom_call" | custom-call | flops 6000000000 | bytes 6000000 | tf_op jit(solution)/shard_map/pallas_call | solution.py:569
  153.8 2.7 %collective-permute-start.15 = (f32[256,128]{1,0:T(8,128)S(1)}, f32[256,128]{1,0:T(8,128)S(1)}, u32[]{:S(2)}, u32[]{:S(2)}) collective-permute-start(f32[256,128]{1,0:T(8,128)S(1)} %get-tuple-element.97), channel_id=1, source_target_pairs={{0,64},{64,128},{128,192},{192,0},{1,65},{65,129},{129,193},{193,1... | collective-permute-start | bytes 393224 | tf_op jit(solution)/shard_map/ppermute | solution.py:451
  156.6 5.2 %collective-permute-start.16 = (f32[256,128]{1,0:T(8,128)S(1)}, f32[256,128]{1,0:T(8,128)S(1)}, u32[]{:S(2)}, u32[]{:S(2)}) collective-permute-start(f32[256,128]{1,0:T(8,128)S(1)} %get-tuple-element.96), channel_id=1, source_target_pairs={{0,128},{64,192},{128,0},{192,64},{1,129},{65,193},{129,1},{193,65... | collective-permute-start | bytes 393224 | tf_op jit(solution)/shard_map/ppermute | solution.py:451
  161.8 4.0 %collective-permute-done.15.refs_1_ = f32[256,128]{1,0:T(8,128)S(1)} collective-permute-done((f32[256,128]{1,0:T(8,128)S(1)}, f32[256,128]{1,0:T(8,128)S(1)}, u32[]{:S(2)}, u32[]{:S(2)}) %collective-permute-start.15) | collective-permute-done | bytes 131104 | tf_op jit(solution)/shard_map/ppermute | solution.py:451
  165.8 2.9 %collective-permute-done.16.refs_2_ = f32[256,128]{1,0:T(8,128)S(1)} collective-permute-done((f32[256,128]{1,0:T(8,128)S(1)}, f32[256,128]{1,0:T(8,128)S(1)}, u32[]{:S(2)}, u32[]{:S(2)}) %collective-permute-start.16) | collective-permute-done | bytes 131104 | tf_op jit(solution)/shard_map/ppermute | solution.py:451
  171.7 25.2 %all_to_all.25.in_ref = f32[32,64,128]{2,1,0:T(8,128)S(1)} all-to-all(f32[32,64,128]{2,1,0:T(8,128)S(1)} %shard_map.138), channel_id=1, replica_groups=mesh['zp'=4,'zl'=2,'x'=4,'y'=4,'core'=2] {'zl','x','y'}, dimensions={0} | all-to-all | bytes 2097152 | tf_op jit(solution)/shard_map/all_to_all | solution.py:577
  (99 shorter events, 28.9 us)
Async XLA Ops:
  10.8 16.2 %collective-permute-start.2 = (f32[2,16,2048]{2,1,0:T(8,128)S(1)}, f32[2,16,2048]{2,1,0:T(8,128)S(1)}, u32[]{:S(2)}, u32[]{:S(2)}) collective-permute-start(f32[2,16,2048]{2,1,0:T(8,128)S(1)} %get-tuple-element.92), channel_id=1, source_target_pairs={{0,6},{2,0},{4,2},{6,4},{1,7},{3,1},{5,3},{7,5},{8,14},{10,8},{12,... | collective-permute-start | bytes 786440 | tf_op jit(solution)/shard_map/ppermute | solution.py:451
  13.8 13.1 %collective-permute-start.1 = (f32[2,16,2048]{2,1,0:T(8,128)S(1)}, f32[2,16,2048]{2,1,0:T(8,128)S(1)}, u32[]{:S(2)}, u32[]{:S(2)}) collective-permute-start(f32[2,16,2048]{2,1,0:T(8,128)S(1)} %get-tuple-element.93), channel_id=1, source_target_pairs={{0,4},{2,6},{4,0},{6,2},{1,5},{3,7},{5,1},{7,3},{8,12},{10,14},{12... | collective-permute-start | bytes 786440 | tf_op jit(solution)/shard_map/ppermute | solution.py:451
  14.5 14.3 %collective-permute-start = (f32[2,16,2048]{2,1,0:T(8,128)S(1)}, f32[2,16,2048]{2,1,0:T(8,128)S(1)}, u32[]{:S(2)}, u32[]{:S(2)}) collective-permute-start(f32[2,16,2048]{2,1,0:T(8,128)S(1)} %get-tuple-element.94), channel_id=1, source_target_pairs={{0,2},{2,4},{4,6},{6,0},{1,3},{3,5},{5,7},{7,1},{8,10},{10,12},{12... | collective-permute-start | bytes 786440 | tf_op jit(solution)/shard_map/ppermute | solution.py:451
  15.5 25.1 %all-to-all-start.1 = ((f32[32,24,128]{2,1,0:T(8,128)}), f32[32,24,128]{2,1,0:T(8,128)S(1)}, u32[]{:S(2)}, u32[]{:S(2)}) async-start(f32[32,24,128]{2,1,0:T(8,128)} %shard_map.131), calls=%async_computation.1 | async-start | bytes 786432 | tf_op jit(solution)/shard_map/all_to_all | solution.py:494
  26.6 79.4 %all-gather.3.cloned.1.call-start = ((), (), s32[]{:S(2)}) async-start(), calls=%async_computation.5 | async-start | bytes 2359296 | tf_op jit(solution)/shard_map/all_gather | solution.py:534
  29.0 36.4 %collective-permute-start.3 = (f32[2,16,2048]{2,1,0:T(8,128)S(1)}, f32[2,16,2048]{2,1,0:T(8,128)S(1)}, u32[]{:S(2)}, u32[]{:S(2)}) collective-permute-start(f32[2,16,2048]{2,1,0:T(8,128)S(1)} %get-tuple-element.89), channel_id=1, source_target_pairs={{0,64},{64,128},{128,192},{192,0},{1,65},{65,129},{129,193},{193,1... | collective-permute-start | bytes 786440 | tf_op jit(solution)/shard_map/ppermute | solution.py:451
  32.3 33.1 %collective-permute-start.4 = (f32[2,16,2048]{2,1,0:T(8,128)S(1)}, f32[2,16,2048]{2,1,0:T(8,128)S(1)}, u32[]{:S(2)}, u32[]{:S(2)}) collective-permute-start(f32[2,16,2048]{2,1,0:T(8,128)S(1)} %get-tuple-element.88), channel_id=1, source_target_pairs={{0,128},{64,192},{128,0},{192,64},{1,129},{65,193},{129,1},{193,65... | collective-permute-start | bytes 786440 | tf_op jit(solution)/shard_map/ppermute | solution.py:451
  36.8 28.6 %collective-permute-start.5 = (f32[2,16,2048]{2,1,0:T(8,128)S(1)}, f32[2,16,2048]{2,1,0:T(8,128)S(1)}, u32[]{:S(2)}, u32[]{:S(2)}) collective-permute-start(f32[2,16,2048]{2,1,0:T(8,128)S(1)} %get-tuple-element.87), channel_id=1, source_target_pairs={{0,192},{64,0},{128,64},{192,128},{1,193},{65,1},{129,65},{193,129... | collective-permute-start | bytes 786440 | tf_op jit(solution)/shard_map/ppermute | solution.py:451
  66.1 10.0 %collective-permute-start.6 = (f32[32,8,128]{2,1,0:T(8,128)S(1)}, f32[32,8,128]{2,1,0:T(8,128)S(1)}, u32[]{:S(2)}, u32[]{:S(2)}) collective-permute-start(f32[32,8,128]{2,1,0:T(8,128)S(1)} %slice.13.refs_0_), channel_id=1, source_target_pairs={{0,64},{64,128},{128,192},{192,0},{1,65},{65,129},{129,193},{193,1... | collective-permute-start | bytes 393224 | tf_op jit(solution)/shard_map/ppermute | solution.py:451
  68.5 8.6 %collective-permute-start.7 = (f32[32,8,128]{2,1,0:T(8,128)S(1)}, f32[32,8,128]{2,1,0:T(8,128)S(1)}, u32[]{:S(2)}, u32[]{:S(2)}) collective-permute-start(f32[32,8,128]{2,1,0:T(8,128)S(1)} %slice.13.refs_0_), channel_id=1, source_target_pairs={{0,192},{64,0},{128,64},{192,128},{1,193},{65,1},{129,65},{193,129... | collective-permute-start | bytes 393224 | tf_op jit(solution)/shard_map/ppermute | solution.py:451
  75.3 16.9 %copy-start = (bf16[2,8,256,256]{3,2,1,0:T(8,128)(2,1)}, bf16[2,8,256,256]{3,2,1,0:T(8,128)(2,1)S(1)}, u32[]{:S(2)}) copy-start(bf16[2,8,256,256]{3,2,1,0:T(8,128)(2,1)S(1)} %pad_maximum_fusion.1.mix_hbm.refs_10_) | copy-start | bytes 6291460
  76.1 6.4 %collective-permute-start.8 = (f32[16,8,128]{2,1,0:T(8,128)S(1)}, f32[16,8,128]{2,1,0:T(8,128)S(1)}, u32[]{:S(2)}, u32[]{:S(2)}) collective-permute-start(f32[16,8,128]{2,1,0:T(8,128)S(1)} %slice.16), channel_id=1, source_target_pairs={{0,64},{64,128},{128,192},{192,0},{1,65},{65,129},{129,193},{193,1... | collective-permute-start | bytes 196616 | tf_op jit(solution)/shard_map/ppermute | solution.py:451
  77.1 6.4 %collective-permute-start.9 = (f32[16,8,128]{2,1,0:T(8,128)S(1)}, f32[16,8,128]{2,1,0:T(8,128)S(1)}, u32[]{:S(2)}, u32[]{:S(2)}) collective-permute-start(f32[16,8,128]{2,1,0:T(8,128)S(1)} %slice.17), channel_id=1, source_target_pairs={{0,192},{64,0},{128,64},{192,128},{1,193},{65,1},{129,65},{193,129... | collective-permute-start | bytes 196616 | tf_op jit(solution)/shard_map/ppermute | solution.py:451
  83.6 2.3 %collective-permute-start.10 = (f32[32,8,128]{2,1,0:T(8,128)S(1)}, f32[32,8,128]{2,1,0:T(8,128)S(1)}, u32[]{:S(2)}, u32[]{:S(2)}) collective-permute-start(f32[32,8,128]{2,1,0:T(8,128)S(1)} %slice.13.refs_0_), channel_id=1, source_target_pairs={{0,1},{1,0},{2,3},{3,2},{4,5},{5,4},{6,7},{7,6},{8,9},{9,8},{10,11... | collective-permute-start | bytes 393224 | tf_op jit(solution)/shard_map/ppermute | solution.py:459
  83.6 2.3 %collective-permute-start.11 = (f32[32,8,128]{2,1,0:T(8,128)S(1)}, f32[32,8,128]{2,1,0:T(8,128)S(1)}, u32[]{:S(2)}, u32[]{:S(2)}) collective-permute-start(f32[32,8,128]{2,1,0:T(8,128)S(1)} %collective-permute-done.6.refs_1_), channel_id=1, source_target_pairs={{0,1},{1,0},{2,3},{3,2},{4,5},{5,4},{6,7},{7,6},{8,9},{9,8},{10,11... | collective-permute-start | bytes 393224 | tf_op jit(solution)/shard_map/ppermute | solution.py:459
  84.1 1.8 collective-permute-start.12
  84.1 1.4 collective-permute-start.13
  84.6 1.3 collective-permute-start.14
  92.2 25.4 %all-to-all-start.3 = ((f32[32,72,128]{2,1,0:T(8,128)}), f32[32,72,128]{2,1,0:T(8,128)S(1)}, u32[]{:S(2)}, u32[]{:S(2)}) async-start(f32[32,72,128]{2,1,0:T(8,128)} %shard_map.134), calls=%async_computation.3 | async-start | bytes 2359296 | tf_op jit(solution)/shard_map/all_to_all | solution.py:545
  117.6 33.0 %all-to-all-start.2 = ((f32[32,128,128]{2,1,0:T(8,128)}), f32[32,128,128]{2,1,0:T(8,128)S(1)}, u32[]{:S(2)}, u32[]{:S(2)}) async-start(f32[32,128,128]{2,1,0:T(8,128)} %shard_map.133), calls=%async_computation.2 | async-start | bytes 4194304 | tf_op jit(solution)/shard_map/all_to_all | solution.py:564
  153.8 12.0 %collective-permute-start.15 = (f32[256,128]{1,0:T(8,128)S(1)}, f32[256,128]{1,0:T(8,128)S(1)}, u32[]{:S(2)}, u32[]{:S(2)}) collective-permute-start(f32[256,128]{1,0:T(8,128)S(1)} %get-tuple-element.97), channel_id=1, source_target_pairs={{0,64},{64,128},{128,192},{192,0},{1,65},{65,129},{129,193},{193,1... | collective-permute-start | bytes 393224 | tf_op jit(solution)/shard_map/ppermute | solution.py:451
  156.6 12.1 %collective-permute-start.16 = (f32[256,128]{1,0:T(8,128)S(1)}, f32[256,128]{1,0:T(8,128)S(1)}, u32[]{:S(2)}, u32[]{:S(2)}) collective-permute-start(f32[256,128]{1,0:T(8,128)S(1)} %get-tuple-element.96), channel_id=1, source_target_pairs={{0,128},{64,192},{128,0},{192,64},{1,129},{65,193},{129,1},{193,65... | collective-permute-start | bytes 393224 | tf_op jit(solution)/shard_map/ppermute | solution.py:451
  161.8 8.4 %collective-permute-start.17 = (f32[256,128]{1,0:T(8,128)S(1)}, f32[256,128]{1,0:T(8,128)S(1)}, u32[]{:S(2)}, u32[]{:S(2)}) collective-permute-start(f32[256,128]{1,0:T(8,128)S(1)} %get-tuple-element.95), channel_id=1, source_target_pairs={{0,192},{64,0},{128,64},{192,128},{1,193},{65,1},{129,65},{193,129... | collective-permute-start | bytes 393224 | tf_op jit(solution)/shard_map/ppermute | solution.py:451
  170.2 1.4 collective-permute-start.18
  (14 other events, 107.9 us)
Sparse Core Ops, SparseCore 0:
  70.5 35.5 all-gather.2
